TPU v7x, 256 devices: a whole 4x4x8 slice. The times are simulated.
256 devices in a mesh: slab: 32 (over z, x), src: 8 (over y, core).
Axes of the slice: x: 4, y: 4, z: 8, core: 2. Of those that a mesh axis runs over, the one named last changes fastest.
Arguments:
- sigma: float32 [128, 128, 128], P('slab'), may hold values from 0.2 to 2
- iterate: float32 [32, 128, 128, 128], P('src', 'slab'), may hold values from -4.5 to 4.5, as said below
- counts: int32 [8], replicated, may hold values from 0 to 4, as said below
- sources: int32 [8, 4], replicated, may hold values from 0 to 2097151
Outputs:
- potential: float32 [32, 128, 128, 128], P('src', 'slab')
- residual: float32 [32, 128, 128, 128], P('src', 'slab')
Inputs may be any that keep to these rules, and one draw needn't show every extreme that they name: counts[g] + counts[(g + 4) % 8] = 4 for every group g, and some group holds 4 live columns in every draw. `iterate`: rough values.
All inputs are finite; a program needn't handle non-finite values.
Results may differ from a plain program's by a relative error of at most 0.0003.
Values sent between devices are 32-bit elements; how exact they have to be, the bound alone decides.
A program may use at most 64 MiB of HBM per device.

v0:
```python
from functools import reduce

import jax
import jax.numpy as jnp
from jax import lax
from jax.sharding import PartitionSpec as P

ITERS = 6


def extended_2(block, sides, width):
    for axis, dim in sides:
        count = lax.axis_size(axis)
        forward = [(i, i + 1) for i in range(count - 1)]
        backward = [(target, source) for source, target in forward]
        low = lax.ppermute(
            lax.slice_in_dim(block, block.shape[dim] - width, None, axis=dim), axis, forward
        )
        high = lax.ppermute(lax.slice_in_dim(block, 0, width, axis=dim), axis, backward)
        block = jnp.concatenate([low, block, high], axis=dim)
    return block


def face(first, second):
    return 2.0 * first * second / (first + second)


def adder(left, right):
    return left + right


def shards(sigma, iterate, counts, sources):
    depth, rows, cols = sigma.shape
    ngroups = counts.shape[0]
    slots_here = iterate.shape[0]
    last_slab = lax.axis_size("slab") - 1
    slab_at = lax.axis_index("slab")
    group_at = lax.axis_index("src")
    rim = extended_2(sigma, (("slab", 0),), 1)
    below = jnp.where(slab_at == 0, sigma[:1], rim[:1])
    above = jnp.where(slab_at == last_slab, sigma[-1:], rim[-1:])
    neighbours = (
        jnp.concatenate([below, sigma[:-1]], 0),
        jnp.concatenate([sigma[1:], above], 0),
        jnp.concatenate([sigma[:, :1], sigma[:, :-1]], 1),
        jnp.concatenate([sigma[:, 1:], sigma[:, -1:]], 1),
        jnp.concatenate([sigma[:, :, :1], sigma[:, :, :-1]], 2),
        jnp.concatenate([sigma[:, :, 1:], sigma[:, :, -1:]], 2),
    )
    weights = tuple((face(sigma, other) for other in neighbours))
    diag = reduce(adder, weights)

    def operate(field):
        extended = extended_2(field, (("slab", 1),), 1)
        edge_x = jnp.zeros_like(field[:, :, :1])
        edge_y = jnp.zeros_like(field[:, :, :, :1])
        beside_all = (
            extended[:, :-2],
            extended[:, 2:],
            jnp.concatenate([edge_x, field[:, :, :-1]], 2),
            jnp.concatenate([field[:, :, 1:], edge_x], 2),
            jnp.concatenate([edge_y, field[:, :, :, :-1]], 3),
            jnp.concatenate([field[:, :, :, 1:], edge_y], 3),
        )
        terms = [weight[None] * other for weight, other in zip(weights, beside_all)]
        return diag[None] * field - reduce(adder, terms)

    def inner(first, second):
        return jnp.sum(first * second, axis=(1, 2, 3))

    def widen(value):
        return value[:, None, None, None]

    def residual_sums(r_now, z_now):
        return lax.psum(inner(r_now, z_now), "slab")

    zi = lax.broadcasted_iota(jnp.int32, (depth, rows, cols), 0)
    xi = lax.broadcasted_iota(jnp.int32, (depth, rows, cols), 1)
    yi = lax.broadcasted_iota(jnp.int32, (depth, rows, cols), 2)
    cell_ids = ((slab_at * depth + zi) * rows + xi) * cols + yi
    group_ids = jnp.arange(ngroups, dtype=jnp.int32)
    mine = group_ids == group_at
    count_here = jnp.sum(jnp.where(mine, counts, 0))
    slot_ids = jnp.arange(slots_here, dtype=jnp.int32)
    live = slot_ids < count_here
    own_sources = jnp.sum(jnp.where(mine[:, None], sources, 0), axis=0)
    x_now = iterate
    r_now = (cell_ids[None] == own_sources[:, None, None, None]).astype(jnp.float32) - operate(
        x_now
    )
    z_now = r_now / diag[None]
    p_now = z_now
    rz_now = residual_sums(r_now, z_now)
    for step in range(ITERS):
        image = operate(p_now)
        alpha = rz_now / lax.psum(inner(p_now, image), "slab")
        x_now = x_now + widen(alpha) * p_now
        r_now = r_now - widen(alpha) * image
        z_now = r_now / diag[None]
        rz_new = residual_sums(r_now, z_now)
        p_now = z_now + widen(rz_new / rz_now) * p_now
        rz_now = rz_new
    potential = jnp.where(widen(live), x_now, iterate)
    residual = jnp.where(widen(live), r_now, jnp.zeros_like(r_now))
    return (potential, residual)


def solution(mesh):
    return jax.shard_map(
        shards,
        mesh=mesh,
        in_specs=(P("slab", None, None), P("src", "slab", None, None), P(), P()),
        out_specs=(P("src", "slab", None, None), P("src", "slab", None, None)),
        check_vma=False,
    )
```

profile of v0, /device:TPU:8, one launch (start us, length us, event | category | flops | bytes accessed | tf_op | source)
XLA Modules:
  0.0 933.0 jit_solution(3140148589460854686)
XLA Ops:
  2.8 4.7 collective-permute-start
  9.4 4.1 collective-permute-start.2
  27.8 4.6 collective-permute-start.4
  36.8 4.8 collective-permute-done.5
  42.9 75.9 %all-reduce.28 = (f32[4]{0:T(128)S(1)}, f32[4]{0:T(128)S(1)}) all-reduce(f32[4]{0:T(128)S(1)} %get-tuple-element.3, f32[4]{0:T(128)S(1)} %get-tuple-element.2), channel_id=1, replica_groups=mesh['slab'=32,'src'=8] {'slab'}, use_global_device_ids=true, to_apply=%region_3.4 | all-reduce | flops 8 | bytes 64 | tf_op jit(solution)/shard_map/psum | solution.py:75
  120.0 69.6 %psum.86 = f32[4]{0:T(128)S(1)} all-reduce(f32[4]{0:T(128)S(1)} %get-tuple-element.24), channel_id=1, replica_groups=mesh['slab'=32,'src'=8] {'slab'}, use_global_device_ids=true, to_apply=%region_7.8 | all-reduce | flops 4 | bytes 32 | tf_op jit(solution)/shard_map/psum | solution.py:75
  191.3 3.9 collective-permute-start.6
  199.2 4.5 collective-permute-done.7
  205.7 69.7 %psum.87 = f32[4]{0:T(128)S(1)} all-reduce(f32[4]{0:T(128)S(1)} %get-tuple-element.22), channel_id=1, replica_groups=mesh['slab'=32,'src'=8] {'slab'}, use_global_device_ids=true, to_apply=%region_9.10 | all-reduce | flops 4 | bytes 32 | tf_op jit(solution)/shard_map/psum | solution.py:96
  277.8 71.5 %psum.88 = f32[4]{0:T(128)S(1)} all-reduce(f32[4]{0:T(128)S(1)} %get-tuple-element.20), channel_id=1, replica_groups=mesh['slab'=32,'src'=8] {'slab'}, use_global_device_ids=true, to_apply=%region_11.12 | all-reduce | flops 4 | bytes 32 | tf_op jit(solution)/shard_map/psum | solution.py:75
  356.9 4.6 collective-permute-done.9
  363.5 69.6 %psum.89 = f32[4]{0:T(128)S(1)} all-reduce(f32[4]{0:T(128)S(1)} %get-tuple-element.18), channel_id=1, replica_groups=mesh['slab'=32,'src'=8] {'slab'}, use_global_device_ids=true, to_apply=%region_13.14 | all-reduce | flops 4 | bytes 32 | tf_op jit(solution)/shard_map/psum | solution.py:96
  435.9 71.6 %psum.90 = f32[4]{0:T(128)S(1)} all-reduce(f32[4]{0:T(128)S(1)} %get-tuple-element.16), channel_id=1, replica_groups=mesh['slab'=32,'src'=8] {'slab'}, use_global_device_ids=true, to_apply=%region_15.16 | all-reduce | flops 4 | bytes 32 | tf_op jit(solution)/shard_map/psum | solution.py:75
  515.1 5.1 collective-permute-done.11
  522.2 75.4 %psum.91 = f32[4]{0:T(128)S(1)} all-reduce(f32[4]{0:T(128)S(1)} %get-tuple-element.14), channel_id=1, replica_groups=mesh['slab'=32,'src'=8] {'slab'}, use_global_device_ids=true, to_apply=%region_17.18 | all-reduce | flops 4 | bytes 32 | tf_op jit(solution)/shard_map/psum | solution.py:96
  600.4 69.7 %psum.92 = f32[4]{0:T(128)S(1)} all-reduce(f32[4]{0:T(128)S(1)} %get-tuple-element.12), channel_id=1, replica_groups=mesh['slab'=32,'src'=8] {'slab'}, use_global_device_ids=true, to_apply=%region_19.20 | all-reduce | flops 4 | bytes 32 | tf_op jit(solution)/shard_map/psum | solution.py:75
  671.7 3.9 collective-permute-start.12
  679.5 5.5 collective-permute-done.13
  687.1 75.3 %psum.93 = f32[4]{0:T(128)S(1)} all-reduce(f32[4]{0:T(128)S(1)} %get-tuple-element.10), channel_id=1, replica_groups=mesh['slab'=32,'src'=8] {'slab'}, use_global_device_ids=true, to_apply=%region_21.22 | all-reduce | flops 4 | bytes 32 | tf_op jit(solution)/shard_map/psum | solution.py:96
  765.2 69.7 %psum.94 = f32[4]{0:T(128)S(1)} all-reduce(f32[4]{0:T(128)S(1)} %get-tuple-element.8), channel_id=1, replica_groups=mesh['slab'=32,'src'=8] {'slab'}, use_global_device_ids=true, to_apply=%region_23.24 | all-reduce | flops 4 | bytes 32 | tf_op jit(solution)/shard_map/psum | solution.py:75
  837.0 4.0 collective-permute-start.14
  844.8 5.6 collective-permute-done.15
  852.4 75.2 %psum.95 = f32[4]{0:T(128)S(1)} all-reduce(f32[4]{0:T(128)S(1)} %get-tuple-element.6), channel_id=1, replica_groups=mesh['slab'=32,'src'=8] {'slab'}, use_global_device_ids=true, to_apply=%region_25.26 | all-reduce | flops 4 | bytes 32 | tf_op jit(solution)/shard_map/psum | solution.py:96
  927.7 5.3 subtract_select_fusion
  (167 shorter events, 77.7 us)
Async XLA Ops:
  1.5 21.1 %collective-permute-start.1 = (f32[1,128,128]{2,1,0:T(8,128)S(1)}, f32[1,128,128]{2,1,0:T(8,128)S(1)}, u32[]{:S(2)}, u32[]{:S(2)}) collective-permute-start(f32[1,128,128]{2,1,0:T(8,128)S(1)} %get-tuple-element.90), channel_id=1, source_target_pairs={{8,0},{16,8},{24,16},{32,24},{40,32},{48,40},{56,48},{64,56},{72,6... | collective-permute-start | bytes 196616 | tf_op jit(solution)/shard_map/ppermute | solution.py:19
  2.8 19.8 %collective-permute-start = (f32[1,128,128]{2,1,0:T(8,128)S(1)}, f32[1,128,128]{2,1,0:T(8,128)S(1)}, u32[]{:S(2)}, u32[]{:S(2)}) collective-permute-start(f32[1,128,128]{2,1,0:T(8,128)S(1)} %get-tuple-element.91), channel_id=1, source_target_pairs={{0,8},{8,16},{16,24},{24,32},{32,40},{40,48},{48,56},{56,64},{64,7... | collective-permute-start | bytes 196616 | tf_op jit(solution)/shard_map/ppermute | solution.py:16
  9.4 15.3 %collective-permute-start.2 = (f32[4,1,128,128]{3,2,1,0:T(8,128)}, f32[4,1,128,128]{3,2,1,0:T(8,128)}, u32[]{:S(2)}, u32[]{:S(2)}) collective-permute-start(f32[4,1,128,128]{3,2,1,0:T(8,128)} %get-tuple-element.72), channel_id=1, source_target_pairs={{0,8},{8,16},{16,24},{24,32},{32,40},{40,48},{48,56},{56,64},{64,7... | collective-permute-start | bytes 786440 | tf_op jit(solution)/shard_map/ppermute | solution.py:16
  13.5 11.2 %collective-permute-start.3 = (f32[4,1,128,128]{3,2,1,0:T(8,128)}, f32[4,1,128,128]{3,2,1,0:T(8,128)}, u32[]{:S(2)}, u32[]{:S(2)}) collective-permute-start(f32[4,1,128,128]{3,2,1,0:T(8,128)} %get-tuple-element.73), channel_id=1, source_target_pairs={{8,0},{16,8},{24,16},{32,24},{40,32},{48,40},{56,48},{64,56},{72,6... | collective-permute-start | bytes 786440 | tf_op jit(solution)/shard_map/ppermute | solution.py:19
  24.6 17.0 %copy-start.21 = (f32[4,128,128]{2,1,0:T(8,128)}, f32[4,128,128]{2,1,0:T(8,128)S(1)}, u32[]{:S(2)}) copy-start(f32[4,128,128]{2,1,0:T(8,128)S(1)} %get-tuple-element.34) | copy-start | bytes 786436
  24.6 17.0 %copy-start.27 = (f32[4,128,128]{2,1,0:T(8,128)}, f32[4,128,128]{2,1,0:T(8,128)S(1)}, u32[]{:S(2)}) copy-start(f32[4,128,128]{2,1,0:T(8,128)S(1)} %get-tuple-element.35) | copy-start | bytes 786436
  24.6 336.9 %copy-start.5 = (f32[4,128,128]{2,1,0:T(8,128)}, f32[4,128,128]{2,1,0:T(8,128)S(1)}, u32[]{:S(2)}) copy-start(f32[4,128,128]{2,1,0:T(8,128)S(1)} %get-tuple-element.30) | copy-start | bytes 786436
  24.6 336.9 %copy-start.9 = (f32[4,128,128]{2,1,0:T(8,128)}, f32[4,128,128]{2,1,0:T(8,128)S(1)}, u32[]{:S(2)}) copy-start(f32[4,128,128]{2,1,0:T(8,128)S(1)} %get-tuple-element.31) | copy-start | bytes 786436
  24.6 336.9 %copy-start.13 = (f32[4,128,128]{2,1,0:T(8,128)}, f32[4,128,128]{2,1,0:T(8,128)S(1)}, u32[]{:S(2)}) copy-start(f32[4,128,128]{2,1,0:T(8,128)S(1)} %get-tuple-element.32) | copy-start | bytes 786436
  24.6 336.9 %copy-start.17 = (f32[4,128,128]{2,1,0:T(8,128)}, f32[4,128,128]{2,1,0:T(8,128)S(1)}, u32[]{:S(2)}) copy-start(f32[4,128,128]{2,1,0:T(8,128)S(1)} %get-tuple-element.33) | copy-start | bytes 786436
  27.4 162.2 %copy-start.3 = (f32[4,4,128,128]{3,2,1,0:T(8,128)}, f32[4,4,128,128]{3,2,1,0:T(8,128)S(1)}, u32[]{:S(2)}) copy-start(f32[4,4,128,128]{3,2,1,0:T(8,128)S(1)} %get-tuple-element.28) | copy-start | bytes 3145732
  27.8 9.0 collective-permute-start.4
  32.4 9.2 collective-permute-start.5
  191.3 7.8 collective-permute-start.6
  195.3 8.4 collective-permute-start.7
  203.7 71.7 %copy-start.33 = (f32[4,4,128,128]{3,2,1,0:T(8,128)S(1)}, f32[4,4,128,128]{3,2,1,0:T(8,128)}, u32[]{:S(2)}) copy-start(f32[4,4,128,128]{3,2,1,0:T(8,128)} %get-tuple-element.25) | copy-start | bytes 3145732
  351.0 5.9 collective-permute-start.8
  353.1 8.4 collective-permute-start.9
  509.3 5.9 collective-permute-start.10
  511.2 9.0 collective-permute-start.11
  671.7 7.8 collective-permute-start.12
  675.7 9.4 %collective-permute-start.13 = (f32[4,1,128,128]{3,2,1,0:T(8,128)S(1)}, f32[4,1,128,128]{3,2,1,0:T(8,128)S(1)}, u32[]{:S(2)}, u32[]{:S(2)}) collective-permute-start(f32[4,1,128,128]{3,2,1,0:T(8,128)S(1)} %get-tuple-element.43), channel_id=1, source_target_pairs={{8,0},{16,8},{24,16},{32,24},{40,32},{48,40},{56,48},{64,56},{72,6... | collective-permute-start | bytes 786440 | tf_op jit(solution)/shard_map/ppermute | solution.py:19
  837.0 7.8 collective-permute-start.14
  841.0 9.4 %collective-permute-start.15 = (f32[4,1,128,128]{3,2,1,0:T(8,128)S(1)}, f32[4,1,128,128]{3,2,1,0:T(8,128)S(1)}, u32[]{:S(2)}, u32[]{:S(2)}) collective-permute-start(f32[4,1,128,128]{3,2,1,0:T(8,128)S(1)} %get-tuple-element.37), channel_id=1, source_target_pairs={{8,0},{16,8},{24,16},{32,24},{40,32},{48,40},{56,48},{64,56},{72,6... | collective-permute-start | bytes 786440 | tf_op jit(solution)/shard_map/ppermute | solution.py:19
  (34 other events, 256.2 us)
where the time goes:
time: 952 us; the launch traced here: 933 us
  blocking collectives  793 us (83%)
  waiting for transfers between devices  43.1 us (5%)
  other arithmetic  41.2 us (4%)
  starting transfers between devices  40.2 us (4%)
  local copies, waits for them, and re-layouts  13.7 us (1%)
    psum x6, blocking collectives, residual_sums(): return lax.psum(inner(r_now, z_now), 'slab')  428 us
    psum x5, blocking collectives, shards(): alpha = rz_now / lax.psum(inner(p_now, image), 'slab')  365 us
    ppermute x8, waiting for transfers between devices, extended_2(): lax.ppermute(lax.slice_in_dim(block, 0, width, axis=dim), axis, backward)  30.1 us
    ppermute x8, starting transfers between devices, extended_2(): lax.ppermute(lax.slice_in_dim(block, block.shape[dim] - width, None, axis...  29 us
    reduce_sum x11, other arithmetic, inner(): return jnp.sum(first * second, axis=(1, 2, 3))  23.1 us
  transfers between devices with their start and end apart: 16, of which 12 were waited for; matrix products, arithmetic and copies ran while one was open for 1% of the time, Pallas kernels for 0%

commit v1 on v0

v1 whole, which is shorter than its diff:
```python
import functools

import jax
import jax.numpy as jnp
from jax import lax
from jax.experimental import pallas as pl
from jax.experimental.pallas import tpu as pltpu
from jax.sharding import PartitionSpec as P

MESH = pl.DeviceIdType.MESH
ITERS = 6
STAGES = ITERS + 1
RING = 4
PAD = 8
CHUNK = 32

A = (-0.1666, -0.13, -0.07, -0.02, -0.02, -0.01)
B = (0.0, 0.373, 0.458, 0.484, 0.487, 0.493, 0.495)

PAIRS = [(i, j) for j in range(STAGES) for i in range(min(j + 1, ITERS))]
SLOT = {pair: at for at, pair in enumerate(PAIRS)}


def face(first, second):
    return 2.0 * first * second / (first + second)


def coefficients(gram):
    zero = jnp.zeros_like(gram(0, 0))
    one = zero + 1.0
    c_r, c_p = [one], [one]
    c_x = [zero] * ITERS
    r_dot = [gram(0, l) for l in range(STAGES)]
    rz = r_dot[0]
    for step in range(ITERS):
        c_q = [zero] * (step + 2)
        for i in range(step + 1):
            c_q[i] = c_q[i] + (1.0 - A[i]) * c_p[i]
            c_q[i + 1] = c_q[i + 1] - B[i + 1] * c_p[i]
            if i:
                c_q[i - 1] = c_q[i - 1] - B[i] * c_p[i]
        q_dot = {
            l: functools.reduce(lambda s, t: s + t, [c_q[i] * gram(i, l) for i in range(step + 2)])
            for l in range(step, ITERS)
        }
        alpha = rz / (c_r[step] * q_dot[step])
        c_x = [c_x[i] + alpha * c_p[i] if i <= step else c_x[i] for i in range(ITERS)]
        c_r = [(c_r[i] if i <= step else zero) - alpha * c_q[i] for i in range(step + 2)]
        if step + 1 < ITERS:
            r_dot = {l: r_dot[l] - alpha * q_dot[l] for l in range(step + 1, ITERS)}
            rz_new = c_r[step + 1] * r_dot[step + 1]
            beta = rz_new / rz
            rz = rz_new
            c_p = [c_r[i] + (beta * c_p[i] if i <= step else zero) for i in range(step + 2)]
    return c_x, c_r


def kernel(
    dims,
    counts, sources, sigma_hbm, x_hbm, pot_hbm, res_hbm,
    sig, x_in, v, halo, sig_halo, weights, diag, recip, rows_acc, x_parts, z_parts, table, pot, res,
    load_sem, out_sem, sig_send, sig_recv, send_sem, recv_sem, xs_send, xs_recv, zs_send, zs_recv,
):
    slabs, ncol, depth, rows = dims
    zs = slabs // RING
    cells = depth * rows
    plane = rows
    slab = lax.axis_index("slab")
    group = lax.axis_index("src")
    here_z, here_x = slab // RING, slab % RING
    left, right = (slab + slabs - 1) % slabs, (slab + 1) % slabs

    def peer(at):
        return (at, group)

    x_peers = [here_z * RING + (here_x + d) % RING for d in range(1, RING)]
    z_peers = [((here_z + d) % zs) * RING + here_x for d in range(1, zs)]
    body = pl.ds(PAD, cells)

    load_sig = pltpu.make_async_copy(sigma_hbm, sig.at[body], load_sem.at[0])
    load_sig.start()
    load_x = [pltpu.make_async_copy(x_hbm.at[c], x_in.at[c, body], load_sem.at[1 + c]) for c in range(ncol)]
    for copy in load_x:
        copy.start()

    barrier = pltpu.get_barrier_semaphore()
    greeted = [left, right] + x_peers + z_peers
    for at in greeted:
        pl.semaphore_signal(barrier, inc=1, device_id=peer(at), device_id_type=MESH)
    pl.semaphore_wait(barrier, len(greeted))

    low_rows, high_rows = pl.ds(0, plane), pl.ds(cells - plane, plane)

    def remote(src, dst, send, recv, at):
        return pltpu.make_async_remote_copy(
            src_ref=src, dst_ref=dst, send_sem=send, recv_sem=recv, device_id=peer(at), device_id_type=MESH
        )

    sig_copies = [
        remote(sigma_hbm.at[high_rows], sig_halo.at[0], sig_send.at[0], sig_recv.at[0], right),
        remote(sigma_hbm.at[low_rows], sig_halo.at[1], sig_send.at[1], sig_recv.at[1], left),
    ]
    for copy in sig_copies:
        copy.start()

    def halo_copies(k, c):
        if k == 0:
            high, low = x_hbm.at[c, high_rows], x_hbm.at[c, low_rows]
        else:
            high = v.at[k - 1, c, pl.ds(PAD + cells - plane, plane)]
            low = v.at[k - 1, c, pl.ds(PAD, plane)]
        return (
            remote(high, halo.at[k, 0, c], send_sem.at[k, 0, c], recv_sem.at[k, 0, c], right),
            remote(low, halo.at[k, 1, c], send_sem.at[k, 1, c], recv_sem.at[k, 1, c], left),
        )

    for c in range(ncol):
        for copy in halo_copies(0, c):
            copy.start()

    blank = jnp.zeros((PAD, 128), jnp.float32)
    for c in range(ncol):
        x_in[c, pl.ds(0, PAD)] = blank
        x_in[c, pl.ds(PAD + cells, PAD)] = blank
        for k in range(STAGES):
            v[k, c, pl.ds(0, PAD)] = blank
            v[k, c, pl.ds(PAD + cells, PAD)] = blank
    sig[pl.ds(0, PAD)] = blank + 1.0
    sig[pl.ds(PAD + cells, PAD)] = blank + 1.0
    rows_acc[...] = jnp.zeros_like(rows_acc)

    load_sig.wait()
    for copy in sig_copies:
        copy.wait_recv()

    lane = lax.broadcasted_iota(jnp.int32, (CHUNK, 128), 1)
    sub = lax.broadcasted_iota(jnp.int32, (CHUNK, 128), 0)
    per_plane = plane // CHUNK

    def start_row(q):
        return pl.multiple_of(q * CHUNK, CHUNK)

    def make_weights(row, below, above, open_below, open_above):
        own = sig[pl.ds(PAD + row, CHUNK)]
        x_at = sub + row % plane
        first_x, last_x = x_at == 0, x_at == plane - 1
        first_y, last_y = lane == 0, lane == 127
        others = (
            (below, open_below),
            (above, open_above),
            (sig[pl.ds(PAD - 1 + row, CHUNK)], first_x),
            (sig[pl.ds(PAD + 1 + row, CHUNK)], last_x),
            (pltpu.roll(own, 1, 1), first_y),
            (pltpu.roll(own, 127, 1), last_y),
        )
        total = None
        inner = []
        for other, outside in others:
            w = face(own, jnp.where(outside, own, other))
            total = w if total is None else total + w
            inner.append(jnp.where(outside, 0.0, w))
        inverse = 1.0 / total
        at = pl.ds(row, CHUNK)
        diag[at] = total
        recip[at] = inverse
        for i, w in enumerate(inner):
            weights[i, at] = w * inverse

    def weight_chunk(z, q):
        row = start_row(z * per_plane + q)
        local = pl.ds(start_row(q), CHUNK)
        below = sig_halo[0, local] if z == 0 else sig[pl.ds(PAD + row - plane, CHUNK)]
        above = sig_halo[1, local] if z == depth - 1 else sig[pl.ds(PAD + row + plane, CHUNK)]
        first = (slab == 0) if z == 0 else False
        last = (slab == slabs - 1) if z == depth - 1 else False
        never = jnp.zeros((CHUNK, 128), jnp.int32)
        open_below = (never + first.astype(jnp.int32)) > 0 if z == 0 else never > 0
        open_above = (never + last.astype(jnp.int32)) > 0 if z == depth - 1 else never > 0
        make_weights(row, below, above, open_below, open_above)

    for z in range(depth):
        lax.fori_loop(0, per_plane, lambda q, _, z=z: (weight_chunk(z, q), 0)[1], 0)

    def stage(k, c):
        def field(at):
            return x_in[c, at] if k == 0 else v[k - 1, c, at]

        cell = sources[group, c] - slab * (cells * 128) if k == 0 else None

        def chunk(row, below, above):
            here = pl.ds(PAD + row, CHUNK)
            at = pl.ds(row, CHUNK)
            mid = field(here)
            image = (
                weights[0, at] * below
                + weights[1, at] * above
                + weights[2, at] * field(pl.ds(PAD - 1 + row, CHUNK))
                + weights[3, at] * field(pl.ds(PAD + 1 + row, CHUNK))
                + weights[4, at] * pltpu.roll(mid, 1, 1)
                + weights[5, at] * pltpu.roll(mid, 127, 1)
            )
            if k == 0:
                ids = (sub + row) * 128 + lane
                new = jnp.where(ids == cell, recip[at], 0.0) + (image - mid)
            else:
                j = k - 1
                new = (1.0 / B[k]) * image + (-A[j] / B[k]) * mid
                if j:
                    new = new + (-B[j] / B[k]) * v[k - 2, c, here]
            v[k, c, here] = new

        def edge(q, _):
            row = start_row(q)
            chunk(row, halo[k, 0, c, pl.ds(row, CHUNK)], field(pl.ds(PAD + row + plane, CHUNK)))
            top = start_row(q + (depth - 1) * per_plane)
            chunk(top, field(pl.ds(PAD + top - plane, CHUNK)), halo[k, 1, c, pl.ds(row, CHUNK)])
            return 0

        lax.fori_loop(0, per_plane, edge, 0)
        if k < ITERS:
            for copy in halo_copies(k + 1, c):
                copy.start()

        def inside(q, _):
            row = start_row(q)
            chunk(row, field(pl.ds(PAD + row - plane, CHUNK)), field(pl.ds(PAD + row + plane, CHUNK)))
            return 0

        lax.fori_loop(per_plane, (depth - 1) * per_plane, inside, 0)

        def dots(q, sums):
            row = start_row(q)
            here = pl.ds(PAD + row, CHUNK)
            scaled = diag[pl.ds(row, CHUNK)] * v[k, c, here]
            out = []
            for i, total in enumerate(sums):
                product = scaled * v[i, c, here]
                for part in range(CHUNK // 8):
                    total = total + product[part * 8:(part + 1) * 8]
                out.append(total)
            return tuple(out)

        count = min(k + 1, ITERS)
        sums = lax.fori_loop(
            0, depth * per_plane, dots, tuple(jnp.zeros((8, 128), jnp.float32) for _ in range(count))
        )
        for i, total in enumerate(sums):
            rows_acc[pl.ds(SLOT[i, k] * ncol + c, 1), :] = jnp.sum(total, axis=0, keepdims=True)

    for k in range(STAGES):
        def column(c, _, k=k):
            if k == 0:
                pltpu.make_async_copy(x_hbm.at[c], x_in.at[c, body], load_sem.at[1 + c]).wait()
            for copy in halo_copies(k, c):
                copy.wait_recv()
            stage(k, c)
            return 0

        lax.fori_loop(0, ncol, column, 0)

    mine = jnp.sum(jnp.transpose(rows_acc[...]), axis=0, keepdims=True)
    x_parts[here_x] = mine
    x_copies = [
        remote(x_parts.at[here_x], x_parts.at[here_x], xs_send.at[d], xs_recv.at[d], at)
        for d, at in enumerate(x_peers)
    ]
    for copy in x_copies:
        copy.start()
    for copy in x_copies:
        copy.wait_recv()
    total = x_parts[0]
    for i in range(1, RING):
        total = total + x_parts[i]
    z_parts[here_z] = total
    z_copies = [
        remote(z_parts.at[here_z], z_parts.at[here_z], zs_send.at[d], zs_recv.at[d], at)
        for d, at in enumerate(z_peers)
    ]
    for copy in z_copies:
        copy.start()
    for copy in z_copies:
        copy.wait_recv()
    total = z_parts[0]
    for i in range(1, zs):
        total = total + z_parts[i]

    wide = jnp.broadcast_to(total, (8, 128))
    entries = {}
    for pair, at in SLOT.items():
        entries[pair] = wide if at == 0 else pltpu.roll(wide, 128 - at * ncol, 1)

    def gram(i, j):
        return entries[(i, j)] if i <= j and (i, j) in entries else entries[(j, i)]

    c_x, c_r = coefficients(gram)
    live = lax.broadcasted_iota(jnp.int32, (8, 128), 1) < counts[group]
    for j, value in enumerate(c_x + c_r):
        value = jnp.where(live, value, 0.0)
        for c in range(ncol):
            table[c, pl.ds(j, 1)] = jnp.broadcast_to(value[:1, c:c + 1], (1, 128))

    for c in range(ncol):
        def combine(q, _, c=c):
            row = start_row(q)
            here, at = pl.ds(PAD + row, CHUNK), pl.ds(row, CHUNK)
            new_x, new_r = x_in[c, here], None
            for j in range(STAGES):
                vec = v[j, c, here]
                if j < ITERS:
                    new_x = new_x + table[c, pl.ds(j, 1)] * vec
                term = table[c, pl.ds(ITERS + j, 1)] * vec
                new_r = term if new_r is None else new_r + term
            pot[c, at] = new_x
            res[c, at] = diag[at] * new_r
            return 0

        lax.fori_loop(0, depth * per_plane, combine, 0)
        pltpu.make_async_copy(pot.at[c], pot_hbm.at[c], out_sem.at[0, c]).start()
        pltpu.make_async_copy(res.at[c], res_hbm.at[c], out_sem.at[1, c]).start()

    for copy in sig_copies + x_copies + z_copies:
        copy.wait_send()
    for k in range(STAGES):
        for c in range(ncol):
            for copy in halo_copies(k, c):
                copy.wait_send()
    for c in range(ncol):
        pltpu.make_async_copy(pot.at[c], pot_hbm.at[c], out_sem.at[0, c]).wait()
        pltpu.make_async_copy(res.at[c], res_hbm.at[c], out_sem.at[1, c]).wait()


def solution(mesh):
    slabs = mesh.shape["slab"]

    def shards(sigma, iterate, counts, sources):
        depth, rows, lanes = sigma.shape
        ncol = iterate.shape[0]
        cells = depth * rows
        f32 = jnp.float32
        vmem = pltpu.VMEM
        dma = pltpu.SemaphoreType.DMA
        zs = slabs // RING
        flat = jax.ShapeDtypeStruct((ncol, cells, lanes), f32)
        potential, residual = pl.pallas_call(
            functools.partial(kernel, (slabs, ncol, depth, rows)),
            out_shape=(flat, flat),
            in_specs=[
                pl.BlockSpec(memory_space=pltpu.SMEM),
                pl.BlockSpec(memory_space=pltpu.SMEM),
                pl.BlockSpec(memory_space=pl.ANY),
                pl.BlockSpec(memory_space=pl.ANY),
            ],
            out_specs=(pl.BlockSpec(memory_space=pl.ANY), pl.BlockSpec(memory_space=pl.ANY)),
            scratch_shapes=[
                vmem((cells + 2 * PAD, lanes), f32),
                vmem((ncol, cells + 2 * PAD, lanes), f32),
                vmem((STAGES, ncol, cells + 2 * PAD, lanes), f32),
                vmem((STAGES, 2, ncol, rows, lanes), f32),
                vmem((2, rows, lanes), f32),
                vmem((6, cells, lanes), f32),
                vmem((cells, lanes), f32),
                vmem((cells, lanes), f32),
                vmem((128, 128), f32),
                vmem((RING, 1, 128), f32),
                vmem((zs, 1, 128), f32),
                vmem((ncol, 16, 128), f32),
                vmem((ncol, cells, lanes), f32),
                vmem((ncol, cells, lanes), f32),
                dma((1 + ncol,)),
                dma((2, ncol)),
                dma((2,)),
                dma((2,)),
                dma((STAGES, 2, ncol)),
                dma((STAGES, 2, ncol)),
                dma((RING - 1,)),
                dma((RING - 1,)),
                dma((zs - 1,)),
                dma((zs - 1,)),
            ],
            compiler_params=pltpu.CompilerParams(
                collective_id=0, has_side_effects=True, vmem_limit_bytes=40 * 1024 * 1024
            ),
        )(counts, sources, sigma.reshape(cells, lanes), iterate.reshape(ncol, cells, lanes))
        return potential.reshape(iterate.shape), residual.reshape(iterate.shape)

    return jax.shard_map(
        shards,
        mesh=mesh,
        in_specs=(P("slab", None, None), P("src", "slab", None, None), P(), P()),
        out_specs=(P("src", "slab", None, None), P("src", "slab", None, None)),
        check_vma=False,
    )
```

time: 952 us -> 72.9 us (0.08); the launches traced: 933 us -> 72.7 us
  blocking collectives: 793 us -> 0 us
  Pallas kernels: 0 us -> 66.6 us
  waiting for transfers between devices: 43.1 us -> 0 us
  other arithmetic: 41.2 us -> 0 us
  starting transfers between devices: 40.2 us -> 0 us
    psum x11 -> x0, blocking collectives: 793 us -> none  [the longest x6 428 us: residual_sums(): return lax.psum(inner(r_now, z_now), 'slab')]
    pallas_call x0 -> x1, Pallas kernels: none -> 66.6 us  [shards(): pl.pallas_call(functools.partial(kernel, (slabs, ncol, depth, rows)), out...]
    ppermute x16 -> x0, waiting for transfers between devices: 43.1 us -> none  [the longest x8 30.1 us: extended_2(): lax.ppermute(lax.slice_in_dim(block, 0, width, axis=dim), axis, backward)]
    ppermute x16 -> x0, starting transfers between devices: 40.2 us -> none  [the longest x8 29 us: extended_2(): lax.ppermute(lax.slice_in_dim(block, block.shape[dim] - width, None, axis...]
    reduce_sum x13 -> x0, other arithmetic: 23.9 us -> none  [the longest x11 23.1 us: inner(): return jnp.sum(first * second, axis=(1, 2, 3))]
    slice x27 -> x0, local copies, waits for them, and re-layouts: 12 us -> none  [the longest x7 3.79 us: operate(): field[:, :, :, :-1]]
  transfers between devices with their start and end apart: 16 -> 0, of which waited for: 12 -> 0; matrix products, arithmetic and copies ran while one was open for 1% -> 0% of each run, Pallas kernels for 0% -> 0%
where the time goes in v1:
time: 72.9 us; the launch traced here: 72.7 us
  Pallas kernels  66.6 us (91%)
  local copies, waits for them, and re-layouts  5.44 us (7%)
    pallas_call x1, Pallas kernels, shards(): pl.pallas_call(functools.partial(kernel, (slabs, ncol, depth, rows)), out...  66.6 us
    unnamed x11, local copies, waits for them, and re-layouts  5.44 us

profile of v1, /device:TPU:8, one launch (start us, length us, event | category | flops | bytes accessed | tf_op | source)
XLA Modules:
  0.0 72.7 jit_solution(16785301517346114499)
XLA Ops:
  0.6 0.0 copy-start.3
  0.6 0.7 copy-done.3
  1.3 0.0 copy-start.2
  1.3 0.1 copy.6.sources
  1.4 0.6 copy-done.2
  2.0 0.0 copy-start
  2.0 1.2 %copy-done = f32[4,4,128,128]{3,2,1,0:T(8,128)S(1)} copy-done((f32[4,4,128,128]{3,2,1,0:T(8,128)S(1)}, f32[4,4,128,128]{3,2,1,0:T(8,128)}, u32[]{:S(2)}) %copy-start) | copy-done | bytes 1048600
  3.2 0.0 copy-start.1
  3.2 0.9 %copy-done.1 = f32[4,128,128]{2,1,0:T(8,128)S(1)} copy-done((f32[4,128,128]{2,1,0:T(8,128)S(1)}, f32[4,128,128]{2,1,0:T(8,128)}, u32[]{:S(2)}) %copy-start.1) | copy-done | bytes 262168
  4.1 66.6 %shard_map.59 = (f32[4,512,128]{2,1,0:T(8,128)S(1)}, f32[4,512,128]{2,1,0:T(8,128)S(1)}) custom-call(s32[8]{0:T(128)S(1)} %copy-done.2, s32[8,4]{1,0:T(8,128)S(1)} %copy.6.sources, f32[512,128]{1,0:T(8,128)S(1)} %bitcast.7, f32[4,512,128]{2,1,0:T(8,128)S(1)} %bitcast.4), custom_call_target="tpu_custom_call" | custom-call | tf_op jit(solution)/shard_map/pallas_call | solution.py:344
  70.8 1.0 %copy.9 = f32[4,4,128,128]{3,2,1,0:T(8,128)} copy(f32[4,4,128,128]{3,2,1,0:T(8,128)S(1)} %bitcast.6) | data formatting | bytes 2097152
  71.7 1.0 %copy.10 = f32[4,4,128,128]{3,2,1,0:T(8,128)} copy(f32[4,4,128,128]{3,2,1,0:T(8,128)S(1)} %bitcast.5) | data formatting | bytes 2097152
Async XLA Ops:
  0.6 0.7 copy-start.3
  1.3 0.7 copy-start.2
  2.0 1.2 %copy-start = (f32[4,4,128,128]{3,2,1,0:T(8,128)S(1)}, f32[4,4,128,128]{3,2,1,0:T(8,128)}, u32[]{:S(2)}) copy-start(f32[4,4,128,128]{3,2,1,0:T(8,128)} %param.5) | copy-start | bytes 3145732
  3.2 0.9 %copy-start.1 = (f32[4,128,128]{2,1,0:T(8,128)S(1)}, f32[4,128,128]{2,1,0:T(8,128)}, u32[]{:S(2)}) copy-start(f32[4,128,128]{2,1,0:T(8,128)} %param.4) | copy-start | bytes 786436

commit v2 on v1

--- a/solution.py
+++ b/solution.py
@@ -12,7 +12,7 @@
 STAGES = ITERS + 1
 RING = 4
 PAD = 8
-CHUNK = 32
+CHUNK = 64
 
 A = (-0.1666, -0.13, -0.07, -0.02, -0.02, -0.01)
 B = (0.0, 0.373, 0.458, 0.484, 0.487, 0.493, 0.495)
@@ -55,11 +55,11 @@
     return c_x, c_r
 
 
-def kernel(
+def basis_kernel(
     dims,
-    counts, sources, sigma_hbm, x_hbm, pot_hbm, res_hbm,
-    sig, x_in, v, halo, sig_halo, weights, diag, recip, rows_acc, x_parts, z_parts, table, pot, res,
-    load_sem, out_sem, sig_send, sig_recv, send_sem, recv_sem, xs_send, xs_recv, zs_send, zs_recv,
+    counts_hbm, sources_hbm, sigma_hbm, x_hbm, x_in, v, diag, table,
+    counts, sources, sig, halo, sig_halo, weights, recip, rows_acc, x_parts, z_parts,
+    load_sem, sig_send, sig_recv, send_sem, recv_sem, xs_send, xs_recv, zs_send, zs_recv,
 ):
     slabs, ncol, depth, rows = dims
     zs = slabs // RING
@@ -81,6 +81,12 @@
     load_sig.start()
     load_x = [pltpu.make_async_copy(x_hbm.at[c], x_in.at[c, body], load_sem.at[1 + c]) for c in range(ncol)]
     for copy in load_x:
+        copy.start()
+    load_ints = [
+        pltpu.make_async_copy(counts_hbm, counts, load_sem.at[1 + ncol]),
+        pltpu.make_async_copy(sources_hbm, sources, load_sem.at[2 + ncol]),
+    ]
+    for copy in load_ints:
         copy.start()
 
     barrier = pltpu.get_barrier_semaphore()
@@ -130,8 +136,6 @@
     rows_acc[...] = jnp.zeros_like(rows_acc)
 
     load_sig.wait()
-    for copy in sig_copies:
-        copy.wait_recv()
 
     lane = lax.broadcasted_iota(jnp.int32, (CHUNK, 128), 1)
     sub = lax.broadcasted_iota(jnp.int32, (CHUNK, 128), 0)
@@ -178,29 +182,36 @@
         open_above = (never + last.astype(jnp.int32)) > 0 if z == depth - 1 else never > 0
         make_weights(row, below, above, open_below, open_above)
 
-    for z in range(depth):
+    for z in [*range(1, depth - 1), 0, depth - 1]:
+        if z == 0:
+            for copy in sig_copies:
+                copy.wait_recv()
         lax.fori_loop(0, per_plane, lambda q, _, z=z: (weight_chunk(z, q), 0)[1], 0)
+    for copy in load_ints:
+        copy.wait()
 
     def stage(k, c):
         def field(at):
             return x_in[c, at] if k == 0 else v[k - 1, c, at]
 
-        cell = sources[group, c] - slab * (cells * 128) if k == 0 else None
-
-        def chunk(row, below, above):
-            here = pl.ds(PAD + row, CHUNK)
-            at = pl.ds(row, CHUNK)
+        cell = sources[c, group] - slab * (cells * 128) if k == 0 else None
+
+        def work(row, below, above):
+            here = pl.ds(PAD + row, plane)
+            at = pl.ds(row, plane)
             mid = field(here)
             image = (
                 weights[0, at] * below
                 + weights[1, at] * above
-                + weights[2, at] * field(pl.ds(PAD - 1 + row, CHUNK))
-                + weights[3, at] * field(pl.ds(PAD + 1 + row, CHUNK))
+                + weights[2, at] * field(pl.ds(PAD - 1 + row, plane))
+                + weights[3, at] * field(pl.ds(PAD + 1 + row, plane))
                 + weights[4, at] * pltpu.roll(mid, 1, 1)
                 + weights[5, at] * pltpu.roll(mid, 127, 1)
             )
             if k == 0:
-                ids = (sub + row) * 128 + lane
+                ids = (
+                    lax.broadcasted_iota(jnp.int32, (plane, 128), 0) + row
+                ) * 128 + lax.broadcasted_iota(jnp.int32, (plane, 128), 1)
                 new = jnp.where(ids == cell, recip[at], 0.0) + (image - mid)
             else:
                 j = k - 1
@@ -208,25 +219,6 @@
                 if j:
                     new = new + (-B[j] / B[k]) * v[k - 2, c, here]
             v[k, c, here] = new
-
-        def edge(q, _):
-            row = start_row(q)
-            chunk(row, halo[k, 0, c, pl.ds(row, CHUNK)], field(pl.ds(PAD + row + plane, CHUNK)))
-            top = start_row(q + (depth - 1) * per_plane)
-            chunk(top, field(pl.ds(PAD + top - plane, CHUNK)), halo[k, 1, c, pl.ds(row, CHUNK)])
-            return 0
-
-        lax.fori_loop(0, per_plane, edge, 0)
-        if k < ITERS:
-            for copy in halo_copies(k + 1, c):
-                copy.start()
-
-        def inside(q, _):
-            row = start_row(q)
-            chunk(row, field(pl.ds(PAD + row - plane, CHUNK)), field(pl.ds(PAD + row + plane, CHUNK)))
-            return 0
-
-        lax.fori_loop(per_plane, (depth - 1) * per_plane, inside, 0)
 
         def dots(q, sums):
             row = start_row(q)
@@ -240,10 +232,28 @@
                 out.append(total)
             return tuple(out)
 
-        count = min(k + 1, ITERS)
-        sums = lax.fori_loop(
-            0, depth * per_plane, dots, tuple(jnp.zeros((8, 128), jnp.float32) for _ in range(count))
-        )
+        def inside(z, _):
+            row = pl.multiple_of(z * plane, plane)
+            work(row, field(pl.ds(PAD + row - plane, plane)), field(pl.ds(PAD + row + plane, plane)))
+            return 0
+
+        lax.fori_loop(1, depth - 1, inside, 0)
+        sums = tuple(jnp.zeros((8, 128), jnp.float32) for _ in range(min(k + 1, ITERS)))
+        sums = lax.fori_loop(per_plane, (depth - 1) * per_plane, dots, sums)
+
+        from_left, from_right = halo_copies(k, c)
+        to_right, to_left = halo_copies(k + 1, c) if k < ITERS else (None, None)
+        from_left.wait_recv()
+        work(0, halo[k, 0, c], field(pl.ds(PAD + plane, plane)))
+        if to_left is not None:
+            to_left.start()
+        from_right.wait_recv()
+        work(cells - plane, field(pl.ds(PAD + cells - 2 * plane, plane)), halo[k, 1, c])
+        if to_right is not None:
+            to_right.start()
+
+        sums = lax.fori_loop(0, per_plane, dots, sums)
+        sums = lax.fori_loop((depth - 1) * per_plane, depth * per_plane, dots, sums)
         for i, total in enumerate(sums):
             rows_acc[pl.ds(SLOT[i, k] * ncol + c, 1), :] = jnp.sum(total, axis=0, keepdims=True)
 
@@ -251,8 +261,6 @@
         def column(c, _, k=k):
             if k == 0:
                 pltpu.make_async_copy(x_hbm.at[c], x_in.at[c, body], load_sem.at[1 + c]).wait()
-            for copy in halo_copies(k, c):
-                copy.wait_recv()
             stage(k, c)
             return 0
 
@@ -299,9 +307,26 @@
         for c in range(ncol):
             table[c, pl.ds(j, 1)] = jnp.broadcast_to(value[:1, c:c + 1], (1, 128))
 
+    for copy in sig_copies + x_copies + z_copies:
+        copy.wait_send()
+    for k in range(STAGES):
+        for c in range(ncol):
+            for copy in halo_copies(k, c):
+                copy.wait_send()
+
+
+def combine_kernel(dims, x_in, v, diag, table, pot_hbm, res_hbm, pot, res, out_sem):
+    ncol, cells = dims
+
+    def out_copies(c):
+        return (
+            pltpu.make_async_copy(pot.at[c], pot_hbm.at[c], out_sem.at[0, c]),
+            pltpu.make_async_copy(res.at[c], res_hbm.at[c], out_sem.at[1, c]),
+        )
+
     for c in range(ncol):
         def combine(q, _, c=c):
-            row = start_row(q)
+            row = pl.multiple_of(q * CHUNK, CHUNK)
             here, at = pl.ds(PAD + row, CHUNK), pl.ds(row, CHUNK)
             new_x, new_r = x_in[c, here], None
             for j in range(STAGES):
@@ -314,19 +339,12 @@
             res[c, at] = diag[at] * new_r
             return 0
 
-        lax.fori_loop(0, depth * per_plane, combine, 0)
-        pltpu.make_async_copy(pot.at[c], pot_hbm.at[c], out_sem.at[0, c]).start()
-        pltpu.make_async_copy(res.at[c], res_hbm.at[c], out_sem.at[1, c]).start()
-
-    for copy in sig_copies + x_copies + z_copies:
-        copy.wait_send()
-    for k in range(STAGES):
-        for c in range(ncol):
-            for copy in halo_copies(k, c):
-                copy.wait_send()
+        lax.fori_loop(0, cells // CHUNK, combine, 0)
+        for copy in out_copies(c):
+            copy.start()
     for c in range(ncol):
-        pltpu.make_async_copy(pot.at[c], pot_hbm.at[c], out_sem.at[0, c]).wait()
-        pltpu.make_async_copy(res.at[c], res_hbm.at[c], out_sem.at[1, c]).wait()
+        for copy in out_copies(c):
+            copy.wait()
 
 
 def solution(mesh):
@@ -336,38 +354,39 @@
         depth, rows, lanes = sigma.shape
         ncol = iterate.shape[0]
         cells = depth * rows
+        zs = slabs // RING
         f32 = jnp.float32
         vmem = pltpu.VMEM
         dma = pltpu.SemaphoreType.DMA
-        zs = slabs // RING
-        flat = jax.ShapeDtypeStruct((ncol, cells, lanes), f32)
-        potential, residual = pl.pallas_call(
-            functools.partial(kernel, (slabs, ncol, depth, rows)),
-            out_shape=(flat, flat),
-            in_specs=[
-                pl.BlockSpec(memory_space=pltpu.SMEM),
-                pl.BlockSpec(memory_space=pltpu.SMEM),
-                pl.BlockSpec(memory_space=pl.ANY),
-                pl.BlockSpec(memory_space=pl.ANY),
-            ],
-            out_specs=(pl.BlockSpec(memory_space=pl.ANY), pl.BlockSpec(memory_space=pl.ANY)),
-            scratch_shapes=[
-                vmem((cells + 2 * PAD, lanes), f32),
+        anywhere = pl.BlockSpec(memory_space=pl.ANY)
+        on_chip = pl.BlockSpec(memory_space=pltpu.VMEM)
+
+        def in_hbm(array):
+            return pltpu.with_memory_space_constraint(array, pltpu.HBM)
+
+        sources = sources.T
+        held = pl.pallas_call(
+            functools.partial(basis_kernel, (slabs, ncol, depth, rows)),
+            out_shape=(
                 vmem((ncol, cells + 2 * PAD, lanes), f32),
                 vmem((STAGES, ncol, cells + 2 * PAD, lanes), f32),
+                vmem((cells, lanes), f32),
+                vmem((ncol, 16, lanes), f32),
+            ),
+            in_specs=[anywhere] * 4,
+            out_specs=(on_chip,) * 4,
+            scratch_shapes=[
+                pltpu.SMEM(counts.shape, jnp.int32),
+                pltpu.SMEM(sources.shape, jnp.int32),
+                vmem((cells + 2 * PAD, lanes), f32),
                 vmem((STAGES, 2, ncol, rows, lanes), f32),
                 vmem((2, rows, lanes), f32),
                 vmem((6, cells, lanes), f32),
                 vmem((cells, lanes), f32),
-                vmem((cells, lanes), f32),
                 vmem((128, 128), f32),
                 vmem((RING, 1, 128), f32),
                 vmem((zs, 1, 128), f32),
-                vmem((ncol, 16, 128), f32),
-                vmem((ncol, cells, lanes), f32),
-                vmem((ncol, cells, lanes), f32),
-                dma((1 + ncol,)),
-                dma((2, ncol)),
+                dma((3 + ncol,)),
                 dma((2,)),
                 dma((2,)),
                 dma((STAGES, 2, ncol)),
@@ -378,9 +397,23 @@
                 dma((zs - 1,)),
             ],
             compiler_params=pltpu.CompilerParams(
-                collective_id=0, has_side_effects=True, vmem_limit_bytes=40 * 1024 * 1024
+                collective_id=0, has_side_effects=True, vmem_limit_bytes=24 * 1024 * 1024
             ),
-        )(counts, sources, sigma.reshape(cells, lanes), iterate.reshape(ncol, cells, lanes))
+        )(
+            in_hbm(counts),
+            in_hbm(sources),
+            in_hbm(sigma.reshape(cells, lanes)),
+            in_hbm(iterate.reshape(ncol, cells, lanes)),
+        )
+        flat = pltpu.HBM((ncol, cells, lanes), f32)
+        potential, residual = pl.pallas_call(
+            functools.partial(combine_kernel, (ncol, cells)),
+            out_shape=(flat, flat),
+            in_specs=[on_chip] * 4,
+            out_specs=(anywhere, anywhere),
+            scratch_shapes=[vmem((ncol, cells, lanes), f32), vmem((ncol, cells, lanes), f32), dma((2, ncol))],
+            compiler_params=pltpu.CompilerParams(vmem_limit_bytes=24 * 1024 * 1024),
+        )(*held)
         return potential.reshape(iterate.shape), residual.reshape(iterate.shape)
 
     return jax.shard_map(

time: 72.9 us -> 65.2 us (0.89)
  local copies, waits for them, and re-layouts: 5.44 us -> 0 us
  Pallas kernels: 66.6 us -> 64.5 us
    unnamed x11 -> x0, local copies, waits for them, and re-layouts: 5.44 us -> none
    pallas_call x1 -> x2, Pallas kernels: 66.6 us -> 64.5 us  [the longest x1 62.5 us: shards(): pl.pallas_call(functools.partial(basis_kernel, (slabs, ncol, depth, rows)...]
where the time goes in v2:
time: 65.2 us; the launch traced here: 65.1 us
  Pallas kernels  64.5 us (99%)
    pallas_call x1, Pallas kernels, shards(): pl.pallas_call(functools.partial(basis_kernel, (slabs, ncol, depth, rows)...  62.5 us
    pallas_call x1, Pallas kernels, shards(): pl.pallas_call(functools.partial(combine_kernel, (ncol, cells)), out_shap...  1.98 us

profile of v2, /device:TPU:8, one launch (start us, length us, event | category | flops | bytes accessed | tf_op | source)
XLA Modules:
  0.0 65.1 jit_solution(1306184756517049294)
XLA Ops:
  0.6 62.5 %shard_map.59 = (f32[4,528,128]{2,1,0:T(8,128)S(1)}, f32[7,4,528,128]{3,2,1,0:T(8,128)S(1)}, f32[512,128]{1,0:T(8,128)S(1)}, f32[4,16,128]{2,1,0:T(8,128)S(1)}) custom-call(s32[8]{0:T(128)} %counts_hbm.1, s32[4,8]{1,0:T(4,128)} %bitcast.7, f32[512,128]{1,0:T(8,128)} %bitcast.6, f32[4,512,128]{2,1,0:T(8,128)} %bitcast.5), custom_call_target="tpu_custom_call" | custom-call | tf_op jit(solution)/shard_map/pallas_call | solution.py:368
  63.1 2.0 %shard_map.60 = (f32[4,512,128]{2,1,0:T(8,128)}, f32[4,512,128]{2,1,0:T(8,128)}) custom-call(f32[4,528,128]{2,1,0:T(8,128)S(1)} %get-tuple-element.8.x_in, f32[7,4,528,128]{3,2,1,0:T(8,128)S(1)} %get-tuple-element.9.v, f32[512,128]{1,0:T(8,128)S(1)} %get-tuple-element.10.diag, f32[4,16,128]{2,1,0:T(8,128)S(1)} %get-tuple-element.11.table), custom_call_target="tpu_custom_call" | custom-call | tf_op jit(solution)/shard_map/pallas_call | solution.py:409

commit v3 on v2

--- a/solution.py
+++ b/solution.py
@@ -10,7 +10,7 @@
 MESH = pl.DeviceIdType.MESH
 ITERS = 6
 STAGES = ITERS + 1
-RING = 4
+CORES = 2
 PAD = 8
 CHUNK = 64
 
@@ -58,24 +58,25 @@
 def basis_kernel(
     dims,
     counts_hbm, sources_hbm, sigma_hbm, x_hbm, x_in, v, diag, table,
-    counts, sources, sig, halo, sig_halo, weights, recip, rows_acc, x_parts, z_parts,
-    load_sem, sig_send, sig_recv, send_sem, recv_sem, xs_send, xs_recv, zs_send, zs_recv,
+    counts, sources, sig, halo, sig_halo, weights, recip, rows_acc, parts,
+    load_sem, sig_send, sig_recv, send_sem, recv_sem, part_send, part_recv,
 ):
     slabs, ncol, depth, rows = dims
-    zs = slabs // RING
     cells = depth * rows
     plane = rows
     slab = lax.axis_index("slab")
     group = lax.axis_index("src")
-    here_z, here_x = slab // RING, slab % RING
+    core = group % CORES
+    twin = group - core + (CORES - 1 - core)
     left, right = (slab + slabs - 1) % slabs, (slab + 1) % slabs
 
-    def peer(at):
-        return (at, group)
-
-    x_peers = [here_z * RING + (here_x + d) % RING for d in range(1, RING)]
-    z_peers = [((here_z + d) % zs) * RING + here_x for d in range(1, zs)]
+    others = [(slab + d) % slabs for d in range(1, slabs)]
     body = pl.ds(PAD, cells)
+
+    barrier = pltpu.get_barrier_semaphore()
+    greeted = [(at, group) for at in others] + [(slab, twin)]
+    for at in greeted:
+        pl.semaphore_signal(barrier, inc=1, device_id=at, device_id_type=MESH)
 
     load_sig = pltpu.make_async_copy(sigma_hbm, sig.at[body], load_sem.at[0])
     load_sig.start()
@@ -89,25 +90,22 @@
     for copy in load_ints:
         copy.start()
 
-    barrier = pltpu.get_barrier_semaphore()
-    greeted = [left, right] + x_peers + z_peers
-    for at in greeted:
-        pl.semaphore_signal(barrier, inc=1, device_id=peer(at), device_id_type=MESH)
     pl.semaphore_wait(barrier, len(greeted))
 
     low_rows, high_rows = pl.ds(0, plane), pl.ds(cells - plane, plane)
 
-    def remote(src, dst, send, recv, at):
+    def remote(src, dst, send, recv, at, of=group):
         return pltpu.make_async_remote_copy(
-            src_ref=src, dst_ref=dst, send_sem=send, recv_sem=recv, device_id=peer(at), device_id_type=MESH
+            src_ref=src, dst_ref=dst, send_sem=send, recv_sem=recv, device_id=(at, of), device_id_type=MESH
         )
 
-    sig_copies = [
-        remote(sigma_hbm.at[high_rows], sig_halo.at[0], sig_send.at[0], sig_recv.at[0], right),
-        remote(sigma_hbm.at[low_rows], sig_halo.at[1], sig_send.at[1], sig_recv.at[1], left),
-    ]
-    for copy in sig_copies:
-        copy.start()
+    edge = pl.ds(pl.multiple_of((1 - core) * (cells - plane), plane), plane)
+    sig_out = remote(
+        sigma_hbm.at[edge], sig_halo.at[core], sig_send.at[0], sig_recv.at[0],
+        (slab + (1 - 2 * core) + slabs) % slabs,
+    )
+    sig_out.start()
+    sig_share = remote(sig_halo.at[core], sig_halo.at[core], sig_send.at[1], sig_recv.at[1], slab, twin)
 
     def halo_copies(k, c):
         if k == 0:
@@ -184,8 +182,9 @@
 
     for z in [*range(1, depth - 1), 0, depth - 1]:
         if z == 0:
-            for copy in sig_copies:
-                copy.wait_recv()
+            sig_out.wait_recv()
+            sig_share.start()
+            sig_share.wait_recv()
         lax.fori_loop(0, per_plane, lambda q, _, z=z: (weight_chunk(z, q), 0)[1], 0)
     for copy in load_ints:
         copy.wait()
@@ -267,30 +266,26 @@
         lax.fori_loop(0, ncol, column, 0)
 
     mine = jnp.sum(jnp.transpose(rows_acc[...]), axis=0, keepdims=True)
-    x_parts[here_x] = mine
-    x_copies = [
-        remote(x_parts.at[here_x], x_parts.at[here_x], xs_send.at[d], xs_recv.at[d], at)
-        for d, at in enumerate(x_peers)
-    ]
-    for copy in x_copies:
+    parts[slab] = mine
+    part_copies = [remote(parts.at[slab], parts.at[slab], part_send, part_recv, at) for at in others]
+    for copy in part_copies:
         copy.start()
-    for copy in x_copies:
-        copy.wait_recv()
-    total = x_parts[0]
-    for i in range(1, RING):
-        total = total + x_parts[i]
-    z_parts[here_z] = total
-    z_copies = [
-        remote(z_parts.at[here_z], z_parts.at[here_z], zs_send.at[d], zs_recv.at[d], at)
-        for d, at in enumerate(z_peers)
-    ]
-    for copy in z_copies:
-        copy.start()
-    for copy in z_copies:
-        copy.wait_recv()
-    total = z_parts[0]
-    for i in range(1, zs):
-        total = total + z_parts[i]
+    sig_out.wait_send()
+    sig_share.wait_send()
+    for k in range(STAGES):
+        def sent(c, _, k=k):
+            for copy in halo_copies(k, c):
+                copy.wait_send()
+            return 0
+
+        lax.fori_loop(0, ncol, sent, 0)
+    every = parts.at[pl.ds(0, slabs - 1)]
+    all_parts = remote(every, every, part_send, part_recv, right)
+    all_parts.wait_recv()
+    terms = [parts[i] for i in range(slabs)]
+    while len(terms) > 1:
+        terms = [sum(terms[i:i + 2][1:], terms[i]) for i in range(0, len(terms), 2)]
+    total = terms[0]
 
     wide = jnp.broadcast_to(total, (8, 128))
     entries = {}
@@ -307,27 +302,23 @@
         for c in range(ncol):
             table[c, pl.ds(j, 1)] = jnp.broadcast_to(value[:1, c:c + 1], (1, 128))
 
-    for copy in sig_copies + x_copies + z_copies:
-        copy.wait_send()
-    for k in range(STAGES):
-        for c in range(ncol):
-            for copy in halo_copies(k, c):
-                copy.wait_send()
+    all_parts.wait_send()
 
 
 def combine_kernel(dims, x_in, v, diag, table, pot_hbm, res_hbm, pot, res, out_sem):
-    ncol, cells = dims
-
-    def out_copies(c):
+    ncol, cells, plane = dims
+
+    def out_copies(c, row):
+        at = pl.ds(row, plane)
         return (
-            pltpu.make_async_copy(pot.at[c], pot_hbm.at[c], out_sem.at[0, c]),
-            pltpu.make_async_copy(res.at[c], res_hbm.at[c], out_sem.at[1, c]),
+            pltpu.make_async_copy(pot.at[c, at], pot_hbm.at[c, at], out_sem.at[0, c, row // plane]),
+            pltpu.make_async_copy(res.at[c, at], res_hbm.at[c, at], out_sem.at[1, c, row // plane]),
         )
 
     for c in range(ncol):
-        def combine(q, _, c=c):
-            row = pl.multiple_of(q * CHUNK, CHUNK)
-            here, at = pl.ds(PAD + row, CHUNK), pl.ds(row, CHUNK)
+        def combine(z, _, c=c):
+            row = pl.multiple_of(z * plane, plane)
+            here, at = pl.ds(PAD + row, plane), pl.ds(row, plane)
             new_x, new_r = x_in[c, here], None
             for j in range(STAGES):
                 vec = v[j, c, here]
@@ -337,14 +328,15 @@
                 new_r = term if new_r is None else new_r + term
             pot[c, at] = new_x
             res[c, at] = diag[at] * new_r
+            for copy in out_copies(c, row):
+                copy.start()
             return 0
 
-        lax.fori_loop(0, cells // CHUNK, combine, 0)
-        for copy in out_copies(c):
-            copy.start()
+        lax.fori_loop(0, cells // plane, combine, 0)
     for c in range(ncol):
-        for copy in out_copies(c):
-            copy.wait()
+        for row in range(0, cells, plane):
+            for copy in out_copies(c, row):
+                copy.wait()
 
 
 def solution(mesh):
@@ -354,7 +346,6 @@
         depth, rows, lanes = sigma.shape
         ncol = iterate.shape[0]
         cells = depth * rows
-        zs = slabs // RING
         f32 = jnp.float32
         vmem = pltpu.VMEM
         dma = pltpu.SemaphoreType.DMA
@@ -384,17 +375,14 @@
                 vmem((6, cells, lanes), f32),
                 vmem((cells, lanes), f32),
                 vmem((128, 128), f32),
-                vmem((RING, 1, 128), f32),
-                vmem((zs, 1, 128), f32),
+                vmem((slabs, 1, 128), f32),
                 dma((3 + ncol,)),
                 dma((2,)),
                 dma((2,)),
                 dma((STAGES, 2, ncol)),
                 dma((STAGES, 2, ncol)),
-                dma((RING - 1,)),
-                dma((RING - 1,)),
-                dma((zs - 1,)),
-                dma((zs - 1,)),
+                dma,
+                dma,
             ],
             compiler_params=pltpu.CompilerParams(
                 collective_id=0, has_side_effects=True, vmem_limit_bytes=24 * 1024 * 1024
@@ -407,11 +395,11 @@
         )
         flat = pltpu.HBM((ncol, cells, lanes), f32)
         potential, residual = pl.pallas_call(
-            functools.partial(combine_kernel, (ncol, cells)),
+            functools.partial(combine_kernel, (ncol, cells, rows)),
             out_shape=(flat, flat),
             in_specs=[on_chip] * 4,
             out_specs=(anywhere, anywhere),
-            scratch_shapes=[vmem((ncol, cells, lanes), f32), vmem((ncol, cells, lanes), f32), dma((2, ncol))],
+            scratch_shapes=[vmem((ncol, cells, lanes), f32), vmem((ncol, cells, lanes), f32), dma((2, ncol, depth))],
             compiler_params=pltpu.CompilerParams(vmem_limit_bytes=24 * 1024 * 1024),
         )(*held)
         return potential.reshape(iterate.shape), residual.reshape(iterate.shape)

time: 65.2 us -> 64 us (0.982)
  Pallas kernels: 64.5 us -> 63.1 us
    pallas_call x1, Pallas kernels: 62.5 us -> 61.2 us  [shards(): pl.pallas_call(functools.partial(basis_kernel, (slabs, ncol, depth, rows)...]
where the time goes in v3:
time: 64 us; the launch traced here: 63.8 us
  Pallas kernels  63.1 us (99%)
  between operations  0.64 us (1%)
    pallas_call x1, Pallas kernels, shards(): pl.pallas_call(functools.partial(basis_kernel, (slabs, ncol, depth, rows)...  61.2 us
    pallas_call x1, Pallas kernels, shards(): pl.pallas_call(functools.partial(combine_kernel, (ncol, cells, rows)), ou...  1.96 us

profile of v3, /device:TPU:8, one launch (start us, length us, event | category | flops | bytes accessed | tf_op | source)
XLA Modules:
  0.0 63.8 jit_solution(8263765194181647648)
XLA Ops:
  0.6 61.2 %shard_map.59 = (f32[4,528,128]{2,1,0:T(8,128)S(1)}, f32[7,4,528,128]{3,2,1,0:T(8,128)S(1)}, f32[512,128]{1,0:T(8,128)S(1)}, f32[4,16,128]{2,1,0:T(8,128)S(1)}) custom-call(s32[8]{0:T(128)} %counts_hbm.1, s32[4,8]{1,0:T(4,128)} %bitcast.7, f32[512,128]{1,0:T(8,128)} %bitcast.6, f32[4,512,128]{2,1,0:T(8,128)} %bitcast.5), custom_call_target="tpu_custom_call" | custom-call | tf_op jit(solution)/shard_map/pallas_call | solution.py:359
  61.8 2.0 %shard_map.60 = (f32[4,512,128]{2,1,0:T(8,128)}, f32[4,512,128]{2,1,0:T(8,128)}) custom-call(f32[4,528,128]{2,1,0:T(8,128)S(1)} %get-tuple-element.8.x_in, f32[7,4,528,128]{3,2,1,0:T(8,128)S(1)} %get-tuple-element.9.v, f32[512,128]{1,0:T(8,128)S(1)} %get-tuple-element.10.diag, f32[4,16,128]{2,1,0:T(8,128)S(1)} %get-tuple-element.11.table), custom_call_target="tpu_custom_call" | custom-call | tf_op jit(solution)/shard_map/pallas_call | solution.py:397

commit v4 on v3

--- a/solution.py
+++ b/solution.py
@@ -10,6 +10,7 @@
 MESH = pl.DeviceIdType.MESH
 ITERS = 6
 STAGES = ITERS + 1
+RING = 4
 CORES = 2
 PAD = 8
 CHUNK = 64
@@ -17,7 +18,7 @@
 A = (-0.1666, -0.13, -0.07, -0.02, -0.02, -0.01)
 B = (0.0, 0.373, 0.458, 0.484, 0.487, 0.493, 0.495)
 
-PAIRS = [(i, j) for j in range(STAGES) for i in range(min(j + 1, ITERS))]
+PAIRS = [(i, j) for j in range(ITERS) for i in range(j + 1)] + [(ITERS - 1, ITERS)]
 SLOT = {pair: at for at, pair in enumerate(PAIRS)}
 
 
@@ -30,7 +31,7 @@
     one = zero + 1.0
     c_r, c_p = [one], [one]
     c_x = [zero] * ITERS
-    r_dot = [gram(0, l) for l in range(STAGES)]
+    r_dot = [gram(0, l) for l in range(ITERS)]
     rz = r_dot[0]
     for step in range(ITERS):
         c_q = [zero] * (step + 2)
@@ -58,7 +59,7 @@
 def basis_kernel(
     dims,
     counts_hbm, sources_hbm, sigma_hbm, x_hbm, x_in, v, diag, table,
-    counts, sources, sig, halo, sig_halo, weights, recip, rows_acc, parts,
+    counts, sources, sig, halo, sig_halo, weights, recip, rows_acc, last_acc, parts,
     load_sem, sig_send, sig_recv, send_sem, recv_sem, part_send, part_recv,
 ):
     slabs, ncol, depth, rows = dims
@@ -70,7 +71,11 @@
     twin = group - core + (CORES - 1 - core)
     left, right = (slab + slabs - 1) % slabs, (slab + 1) % slabs
 
-    others = [(slab + d) % slabs for d in range(1, slabs)]
+    deep = slabs // RING
+    here_z, here_x = slab // RING, slab % RING
+    steps = [(dz, dx) for dz in range(deep) for dx in range(RING) if dz or dx]
+    steps.sort(key=lambda step: -min(step[0], deep - step[0]) - min(step[1], RING - step[1]))
+    others = [((here_z + dz) % deep) * RING + (here_x + dx) % RING for dz, dx in steps]
     body = pl.ds(PAD, cells)
 
     barrier = pltpu.get_barrier_semaphore()
@@ -132,6 +137,7 @@
     sig[pl.ds(0, PAD)] = blank + 1.0
     sig[pl.ds(PAD + cells, PAD)] = blank + 1.0
     rows_acc[...] = jnp.zeros_like(rows_acc)
+    last_acc[...] = jnp.zeros_like(last_acc)
 
     load_sig.wait()
 
@@ -142,50 +148,63 @@
     def start_row(q):
         return pl.multiple_of(q * CHUNK, CHUNK)
 
-    def make_weights(row, below, above, open_below, open_above):
+    def set_weights(at, total, inner):
+        inverse = 1.0 / total
+        diag[at] = total
+        recip[at] = inverse
+        for i, w in enumerate(inner):
+            weights[i, at] = w * inverse
+
+    def weight_chunk(z, q):
+        row = start_row(z * per_plane + q)
+        at = pl.ds(row, CHUNK)
         own = sig[pl.ds(PAD + row, CHUNK)]
         x_at = sub + row % plane
         first_x, last_x = x_at == 0, x_at == plane - 1
         first_y, last_y = lane == 0, lane == 127
-        others = (
-            (below, open_below),
-            (above, open_above),
+        others = [
+            None if z == 0 else (sig[pl.ds(PAD + row - plane, CHUNK)], None),
+            None if z == depth - 1 else (sig[pl.ds(PAD + row + plane, CHUNK)], None),
             (sig[pl.ds(PAD - 1 + row, CHUNK)], first_x),
             (sig[pl.ds(PAD + 1 + row, CHUNK)], last_x),
             (pltpu.roll(own, 1, 1), first_y),
             (pltpu.roll(own, 127, 1), last_y),
-        )
+        ]
         total = None
-        inner = []
-        for other, outside in others:
-            w = face(own, jnp.where(outside, own, other))
+        inner = {}
+        for i, pair in enumerate(others):
+            if pair is None:
+                continue
+            other, outside = pair
+            w = face(own, other if outside is None else jnp.where(outside, own, other))
             total = w if total is None else total + w
-            inner.append(jnp.where(outside, 0.0, w))
-        inverse = 1.0 / total
+            inner[i] = w if outside is None else jnp.where(outside, 0.0, w)
+        if 0 < z < depth - 1:
+            set_weights(at, total, [inner[i] for i in range(6)])
+        else:
+            diag[at] = total
+            for i, w in inner.items():
+                weights[i, at] = w
+
+    def finish_chunk(z, q):
+        side = 0 if z == 0 else 1
+        row = start_row(z * per_plane + q)
         at = pl.ds(row, CHUNK)
-        diag[at] = total
-        recip[at] = inverse
-        for i, w in enumerate(inner):
-            weights[i, at] = w * inverse
-
-    def weight_chunk(z, q):
-        row = start_row(z * per_plane + q)
-        local = pl.ds(start_row(q), CHUNK)
-        below = sig_halo[0, local] if z == 0 else sig[pl.ds(PAD + row - plane, CHUNK)]
-        above = sig_halo[1, local] if z == depth - 1 else sig[pl.ds(PAD + row + plane, CHUNK)]
-        first = (slab == 0) if z == 0 else False
-        last = (slab == slabs - 1) if z == depth - 1 else False
-        never = jnp.zeros((CHUNK, 128), jnp.int32)
-        open_below = (never + first.astype(jnp.int32)) > 0 if z == 0 else never > 0
-        open_above = (never + last.astype(jnp.int32)) > 0 if z == depth - 1 else never > 0
-        make_weights(row, below, above, open_below, open_above)
-
-    for z in [*range(1, depth - 1), 0, depth - 1]:
-        if z == 0:
-            sig_out.wait_recv()
-            sig_share.start()
-            sig_share.wait_recv()
+        own = sig[pl.ds(PAD + row, CHUNK)]
+        end = (slab == (0 if side == 0 else slabs - 1)).astype(jnp.int32)
+        outside = (jnp.zeros((CHUNK, 128), jnp.int32) + end) > 0
+        w = face(own, jnp.where(outside, own, sig_halo[side, pl.ds(start_row(q), CHUNK)]))
+        inner = [weights[i, at] for i in range(6) if i != side]
+        inner.insert(side, jnp.where(outside, 0.0, w))
+        set_weights(at, diag[at] + w, inner)
+
+    for z in [0, depth - 1, *range(1, depth - 1)]:
         lax.fori_loop(0, per_plane, lambda q, _, z=z: (weight_chunk(z, q), 0)[1], 0)
+    sig_out.wait_recv()
+    sig_share.start()
+    sig_share.wait_recv()
+    for z in (0, depth - 1):
+        lax.fori_loop(0, per_plane, lambda q, _, z=z: (finish_chunk(z, q), 0)[1], 0)
     for copy in load_ints:
         copy.wait()
 
@@ -193,6 +212,7 @@
         def field(at):
             return x_in[c, at] if k == 0 else v[k - 1, c, at]
 
+        firsts = range(k + 1) if k < ITERS else (ITERS - 1,)
         cell = sources[c, group] - slab * (cells * 128) if k == 0 else None
 
         def work(row, below, above):
@@ -224,7 +244,7 @@
             here = pl.ds(PAD + row, CHUNK)
             scaled = diag[pl.ds(row, CHUNK)] * v[k, c, here]
             out = []
-            for i, total in enumerate(sums):
+            for i, total in zip(firsts, sums):
                 product = scaled * v[i, c, here]
                 for part in range(CHUNK // 8):
                     total = total + product[part * 8:(part + 1) * 8]
@@ -237,7 +257,7 @@
             return 0
 
         lax.fori_loop(1, depth - 1, inside, 0)
-        sums = tuple(jnp.zeros((8, 128), jnp.float32) for _ in range(min(k + 1, ITERS)))
+        sums = tuple(jnp.zeros((8, 128), jnp.float32) for _ in firsts)
         sums = lax.fori_loop(per_plane, (depth - 1) * per_plane, dots, sums)
 
         from_left, from_right = halo_copies(k, c)
@@ -253,10 +273,17 @@
 
         sums = lax.fori_loop(0, per_plane, dots, sums)
         sums = lax.fori_loop((depth - 1) * per_plane, depth * per_plane, dots, sums)
-        for i, total in enumerate(sums):
-            rows_acc[pl.ds(SLOT[i, k] * ncol + c, 1), :] = jnp.sum(total, axis=0, keepdims=True)
+        for i, total in zip(firsts, sums):
+            row = jnp.sum(total, axis=0, keepdims=True)
+            if k < ITERS:
+                rows_acc[pl.ds(SLOT[i, k] * ncol + c, 1), :] = row
+            else:
+                last_acc[pl.ds(c, 1), :] = row
 
     for k in range(STAGES):
+        if k == ITERS:
+            mine = jnp.sum(jnp.transpose(rows_acc[...]), axis=0, keepdims=True)
+
         def column(c, _, k=k):
             if k == 0:
                 pltpu.make_async_copy(x_hbm.at[c], x_in.at[c, body], load_sem.at[1 + c]).wait()
@@ -265,8 +292,11 @@
 
         lax.fori_loop(0, ncol, column, 0)
 
-    mine = jnp.sum(jnp.transpose(rows_acc[...]), axis=0, keepdims=True)
-    parts[slab] = mine
+    spot = SLOT[ITERS - 1, ITERS] * ncol + lax.broadcasted_iota(jnp.int32, (8, 128), 0)
+    last = jnp.where(
+        lax.broadcasted_iota(jnp.int32, (8, 128), 1) == spot, jnp.sum(last_acc[...], axis=1, keepdims=True), 0.0
+    )
+    parts[slab] = mine + jnp.sum(last, axis=0, keepdims=True)
     part_copies = [remote(parts.at[slab], parts.at[slab], part_send, part_recv, at) for at in others]
     for copy in part_copies:
         copy.start()
@@ -375,6 +405,7 @@
                 vmem((6, cells, lanes), f32),
                 vmem((cells, lanes), f32),
                 vmem((128, 128), f32),
+                vmem((8, 128), f32),
                 vmem((slabs, 1, 128), f32),
                 dma((3 + ncol,)),
                 dma((2,)),

time: 64 us -> 63.2 us (0.988)
  no operation moved by 1% of the time
where the time goes in v4:
time: 63.2 us; the launch traced here: 63.1 us
  Pallas kernels  62.5 us (99%)
  between operations  0.64 us (1%)
    pallas_call x1, Pallas kernels, shards(): pl.pallas_call(functools.partial(basis_kernel, (slabs, ncol, depth, rows)...  60.5 us
    pallas_call x1, Pallas kernels, shards(): pl.pallas_call(functools.partial(combine_kernel, (ncol, cells, rows)), ou...  1.96 us

profile of v4, /device:TPU:8, one launch (start us, length us, event | category | flops | bytes accessed | tf_op | source)
XLA Modules:
  0.0 63.1 jit_solution(18275131759791815697)
XLA Ops:
  0.6 60.5 %shard_map.59 = (f32[4,528,128]{2,1,0:T(8,128)S(1)}, f32[7,4,528,128]{3,2,1,0:T(8,128)S(1)}, f32[512,128]{1,0:T(8,128)S(1)}, f32[4,16,128]{2,1,0:T(8,128)S(1)}) custom-call(s32[8]{0:T(128)} %counts_hbm.1, s32[4,8]{1,0:T(4,128)} %bitcast.7, f32[512,128]{1,0:T(8,128)} %bitcast.6, f32[4,512,128]{2,1,0:T(8,128)} %bitcast.5), custom_call_target="tpu_custom_call" | custom-call | tf_op jit(solution)/shard_map/pallas_call | solution.py:389
  61.2 2.0 %shard_map.60 = (f32[4,512,128]{2,1,0:T(8,128)}, f32[4,512,128]{2,1,0:T(8,128)}) custom-call(f32[4,528,128]{2,1,0:T(8,128)S(1)} %get-tuple-element.8.x_in, f32[7,4,528,128]{3,2,1,0:T(8,128)S(1)} %get-tuple-element.9.v, f32[512,128]{1,0:T(8,128)S(1)} %get-tuple-element.10.diag, f32[4,16,128]{2,1,0:T(8,128)S(1)} %get-tuple-element.11.table), custom_call_target="tpu_custom_call" | custom-call | tf_op jit(solution)/shard_map/pallas_call | solution.py:428

commit v5 on v4

--- a/solution.py
+++ b/solution.py
@@ -60,7 +60,7 @@
     dims,
     counts_hbm, sources_hbm, sigma_hbm, x_hbm, x_in, v, diag, table,
     counts, sources, sig, halo, sig_halo, weights, recip, rows_acc, last_acc, parts,
-    load_sem, sig_send, sig_recv, send_sem, recv_sem, part_send, part_recv,
+    load_sem, sig_send, sig_recv, send_sem, recv_sem, part_send, part_recv, known_sem,
 ):
     slabs, ncol, depth, rows = dims
     cells = depth * rows
@@ -79,7 +79,7 @@
     body = pl.ds(PAD, cells)
 
     barrier = pltpu.get_barrier_semaphore()
-    greeted = [(at, group) for at in others] + [(slab, twin)]
+    greeted = [(left, group), (right, group), (slab, twin)]
     for at in greeted:
         pl.semaphore_signal(barrier, inc=1, device_id=at, device_id_type=MESH)
 
@@ -280,7 +280,22 @@
             else:
                 last_acc[pl.ds(c, 1), :] = row
 
+    reach = [4]
+    while 2 * reach[-1] < slabs:
+        reach.append(2 * reach[-1])
+    rounds = reach[:-1]
+
     for k in range(STAGES):
+        at_round = k - 4
+        if 1 <= at_round <= len(rounds):
+            for side in range(2):
+                pl.semaphore_wait(known_sem.at[at_round - 1, side], 1)
+        if 0 <= at_round < len(rounds):
+            for side, far in enumerate((rounds[at_round], slabs - rounds[at_round])):
+                pl.semaphore_signal(
+                    known_sem.at[at_round, side], inc=1,
+                    device_id=((slab + far) % slabs, group), device_id_type=MESH,
+                )
         if k == ITERS:
             mine = jnp.sum(jnp.transpose(rows_acc[...]), axis=0, keepdims=True)
 
@@ -414,6 +429,7 @@
                 dma((STAGES, 2, ncol)),
                 dma,
                 dma,
+                pltpu.SemaphoreType.REGULAR((2, 2)),
             ],
             compiler_params=pltpu.CompilerParams(
                 collective_id=0, has_side_effects=True, vmem_limit_bytes=24 * 1024 * 1024

time: 63.2 us -> 61 us (0.965)
  Pallas kernels: 62.5 us -> 60.3 us
    pallas_call x1, Pallas kernels: 60.5 us -> 58.4 us  [shards(): pl.pallas_call(functools.partial(basis_kernel, (slabs, ncol, depth, rows)...]
where the time goes in v5:
time: 61 us
  Pallas kernels  60.3 us (99%)
  between operations  0.64 us (1%)
    pallas_call x1, Pallas kernels, shards(): pl.pallas_call(functools.partial(basis_kernel, (slabs, ncol, depth, rows)...  58.4 us
    pallas_call x1, Pallas kernels, shards(): pl.pallas_call(functools.partial(combine_kernel, (ncol, cells, rows)), ou...  1.96 us

profile of v5, /device:TPU:8, one launch (start us, length us, event | category | flops | bytes accessed | tf_op | source)
XLA Modules:
  0.0 61.0 jit_solution(7409136181749585247)
XLA Ops:
  0.6 58.4 %shard_map.59 = (f32[4,528,128]{2,1,0:T(8,128)S(1)}, f32[7,4,528,128]{3,2,1,0:T(8,128)S(1)}, f32[512,128]{1,0:T(8,128)S(1)}, f32[4,16,128]{2,1,0:T(8,128)S(1)}) custom-call(s32[8]{0:T(128)} %counts_hbm.1, s32[4,8]{1,0:T(4,128)} %bitcast.7, f32[512,128]{1,0:T(8,128)} %bitcast.6, f32[4,512,128]{2,1,0:T(8,128)} %bitcast.5), custom_call_target="tpu_custom_call" | custom-call | tf_op jit(solution)/shard_map/pallas_call | solution.py:404
  59.0 2.0 %shard_map.60 = (f32[4,512,128]{2,1,0:T(8,128)}, f32[4,512,128]{2,1,0:T(8,128)}) custom-call(f32[4,528,128]{2,1,0:T(8,128)S(1)} %get-tuple-element.8.x_in, f32[7,4,528,128]{3,2,1,0:T(8,128)S(1)} %get-tuple-element.9.v, f32[512,128]{1,0:T(8,128)S(1)} %get-tuple-element.10.diag, f32[4,16,128]{2,1,0:T(8,128)S(1)} %get-tuple-element.11.table), custom_call_target="tpu_custom_call" | custom-call | tf_op jit(solution)/shard_map/pallas_call | solution.py:444

commit v6 on v5

--- a/solution.py
+++ b/solution.py
@@ -59,7 +59,7 @@
 def basis_kernel(
     dims,
     counts_hbm, sources_hbm, sigma_hbm, x_hbm, x_in, v, diag, table,
-    counts, sources, sig, halo, sig_halo, weights, recip, rows_acc, last_acc, parts,
+    counts, sources, sig, halo, sig_halo, weights, recip, rows_acc, last_acc, held_acc, parts,
     load_sem, sig_send, sig_recv, send_sem, recv_sem, part_send, part_recv, known_sem,
 ):
     slabs, ncol, depth, rows = dims
@@ -212,7 +212,7 @@
         def field(at):
             return x_in[c, at] if k == 0 else v[k - 1, c, at]
 
-        firsts = range(k + 1) if k < ITERS else (ITERS - 1,)
+        firsts = range(k + 1)
         cell = sources[c, group] - slab * (cells * 128) if k == 0 else None
 
         def work(row, below, above):
@@ -261,24 +261,75 @@
         sums = lax.fori_loop(per_plane, (depth - 1) * per_plane, dots, sums)
 
         from_left, from_right = halo_copies(k, c)
-        to_right, to_left = halo_copies(k + 1, c) if k < ITERS else (None, None)
+        to_right, to_left = halo_copies(k + 1, c)
         from_left.wait_recv()
         work(0, halo[k, 0, c], field(pl.ds(PAD + plane, plane)))
-        if to_left is not None:
+        if k == ITERS - 1:
+            pl.when(c != ncol - 2)(lambda: to_left.start())
+
+            @pl.when(c == ncol - 1)
+            def _():
+                halo_copies(k + 1, ncol - 2)[1].start()
+
+        else:
             to_left.start()
         from_right.wait_recv()
         work(cells - plane, field(pl.ds(PAD + cells - 2 * plane, plane)), halo[k, 1, c])
-        if to_right is not None:
-            to_right.start()
+        to_right.start()
 
         sums = lax.fori_loop(0, per_plane, dots, sums)
         sums = lax.fori_loop((depth - 1) * per_plane, depth * per_plane, dots, sums)
         for i, total in zip(firsts, sums):
             row = jnp.sum(total, axis=0, keepdims=True)
-            if k < ITERS:
-                rows_acc[pl.ds(SLOT[i, k] * ncol + c, 1), :] = row
-            else:
-                last_acc[pl.ds(c, 1), :] = row
+            rows_acc[pl.ds(SLOT[i, k] * ncol + c, 1), :] = row
+
+    def fold(array):
+        total = array[0:8]
+        for part in range(8, plane, 8):
+            total = total + array[part:part + 8]
+        return total
+
+    def last_plane(c, row, below, above):
+        here, at = pl.ds(PAD + row, plane), pl.ds(row, plane)
+        mid = v[ITERS - 1, c, here]
+        image = (
+            weights[2, at] * v[ITERS - 1, c, pl.ds(PAD - 1 + row, plane)]
+            + weights[3, at] * v[ITERS - 1, c, pl.ds(PAD + 1 + row, plane)]
+            + weights[4, at] * pltpu.roll(mid, 1, 1)
+            + weights[5, at] * pltpu.roll(mid, 127, 1)
+        )
+        if below:
+            image = image + weights[0, at] * v[ITERS - 1, c, pl.ds(PAD + row - plane, plane)]
+        if above:
+            image = image + weights[1, at] * v[ITERS - 1, c, pl.ds(PAD + row + plane, plane)]
+        v[ITERS, c, here] = (
+            (1.0 / B[ITERS]) * image
+            + (-A[ITERS - 1] / B[ITERS]) * mid
+            + (-B[ITERS - 1] / B[ITERS]) * v[ITERS - 2, c, here]
+        )
+        held_acc[c] = held_acc[c] + fold(diag[at] * mid * image)
+
+    def last_inner(c, _):
+        held_acc[c] = jnp.zeros((8, 128), jnp.float32)
+        last_plane(c, 0, False, True)
+
+        def inside(z, _):
+            last_plane(c, pl.multiple_of(z * plane, plane), True, True)
+            return 0
+
+        lax.fori_loop(1, depth - 1, inside, 0)
+        last_plane(c, cells - plane, True, False)
+        return 0
+
+    def last_edge(c, side, summed):
+        halo_copies(ITERS, c)[side].wait_recv()
+        row = 0 if side == 0 else cells - plane
+        here, at = pl.ds(PAD + row, plane), pl.ds(row, plane)
+        outer = weights[side, at] * halo[ITERS, side, c]
+        v[ITERS, c, here] = v[ITERS, c, here] + (1.0 / B[ITERS]) * outer
+        if summed:
+            total = held_acc[c] + 2.0 * fold(diag[at] * v[ITERS - 1, c, here] * outer)
+            last_acc[pl.ds(c, 1), :] = jnp.sum(total, axis=0, keepdims=True)
 
     reach = [4]
     while 2 * reach[-1] < slabs:
@@ -298,6 +349,10 @@
                 )
         if k == ITERS:
             mine = jnp.sum(jnp.transpose(rows_acc[...]), axis=0, keepdims=True)
+            lax.fori_loop(0, ncol, last_inner, 0)
+            lax.fori_loop(0, ncol - 1, lambda c, _: (last_edge(c, 0, True), 0)[1], 0)
+            last_edge(ncol - 1, 1, True)
+            break
 
         def column(c, _, k=k):
             if k == 0:
@@ -315,6 +370,8 @@
     part_copies = [remote(parts.at[slab], parts.at[slab], part_send, part_recv, at) for at in others]
     for copy in part_copies:
         copy.start()
+    last_edge(ncol - 1, 0, False)
+    lax.fori_loop(0, ncol - 1, lambda c, _: (last_edge(c, 1, False), 0)[1], 0)
     sig_out.wait_send()
     sig_share.wait_send()
     for k in range(STAGES):
@@ -336,6 +393,12 @@
     entries = {}
     for pair, at in SLOT.items():
         entries[pair] = wide if at == 0 else pltpu.roll(wide, 128 - at * ncol, 1)
+
+    entries[(ITERS - 1, ITERS)] = (
+        entries[(ITERS - 1, ITERS)]
+        - A[ITERS - 1] * entries[(ITERS - 1, ITERS - 1)]
+        - B[ITERS - 1] * entries[(ITERS - 2, ITERS - 1)]
+    ) / B[ITERS]
 
     def gram(i, j):
         return entries[(i, j)] if i <= j and (i, j) in entries else entries[(j, i)]
@@ -421,6 +484,7 @@
                 vmem((cells, lanes), f32),
                 vmem((128, 128), f32),
                 vmem((8, 128), f32),
+                vmem((ncol, 8, 128), f32),
                 vmem((slabs, 1, 128), f32),
                 dma((3 + ncol,)),
                 dma((2,)),

time: 61 us -> 60.6 us (level)
  no operation moved by 1% of the time
where the time goes in v6:
time: 60.6 us; the launch traced here: 60.5 us
  Pallas kernels  59.8 us (99%)
  between operations  0.64 us (1%)
    pallas_call x1, Pallas kernels, shards(): pl.pallas_call(functools.partial(basis_kernel, (slabs, ncol, depth, rows)...  57.9 us
    pallas_call x1, Pallas kernels, shards(): pl.pallas_call(functools.partial(combine_kernel, (ncol, cells, rows)), ou...  1.96 us

profile of v6, /device:TPU:8, one launch (start us, length us, event | category | flops | bytes accessed | tf_op | source)
XLA Modules:
  0.0 60.5 jit_solution(66019154711394732)
XLA Ops:
  0.6 57.9 %shard_map.59 = (f32[4,528,128]{2,1,0:T(8,128)S(1)}, f32[7,4,528,128]{3,2,1,0:T(8,128)S(1)}, f32[512,128]{1,0:T(8,128)S(1)}, f32[4,16,128]{2,1,0:T(8,128)S(1)}) custom-call(s32[8]{0:T(128)} %counts_hbm.1, s32[4,8]{1,0:T(4,128)} %bitcast.7, f32[512,128]{1,0:T(8,128)} %bitcast.6, f32[4,512,128]{2,1,0:T(8,128)} %bitcast.5), custom_call_target="tpu_custom_call" | custom-call | tf_op jit(solution)/shard_map/pallas_call | solution.py:467
  58.5 2.0 %shard_map.60 = (f32[4,512,128]{2,1,0:T(8,128)}, f32[4,512,128]{2,1,0:T(8,128)}) custom-call(f32[4,528,128]{2,1,0:T(8,128)S(1)} %get-tuple-element.8.x_in, f32[7,4,528,128]{3,2,1,0:T(8,128)S(1)} %get-tuple-element.9.v, f32[512,128]{1,0:T(8,128)S(1)} %get-tuple-element.10.diag, f32[4,16,128]{2,1,0:T(8,128)S(1)} %get-tuple-element.11.table), custom_call_target="tpu_custom_call" | custom-call | tf_op jit(solution)/shard_map/pallas_call | solution.py:508

commit v7 on v6

--- a/solution.py
+++ b/solution.py
@@ -309,6 +309,10 @@
         )
         held_acc[c] = held_acc[c] + fold(diag[at] * mid * image)
 
+    def sent(k, c):
+        for copy in halo_copies(k, c):
+            copy.wait_send()
+
     def last_inner(c, _):
         held_acc[c] = jnp.zeros((8, 128), jnp.float32)
         last_plane(c, 0, False, True)
@@ -350,6 +354,8 @@
         if k == ITERS:
             mine = jnp.sum(jnp.transpose(rows_acc[...]), axis=0, keepdims=True)
             lax.fori_loop(0, ncol, last_inner, 0)
+            for done in range(ITERS):
+                lax.fori_loop(0, ncol, lambda c, _, done=done: (sent(done, c), 0)[1], 0)
             lax.fori_loop(0, ncol - 1, lambda c, _: (last_edge(c, 0, True), 0)[1], 0)
             last_edge(ncol - 1, 1, True)
             break
@@ -374,13 +380,7 @@
     lax.fori_loop(0, ncol - 1, lambda c, _: (last_edge(c, 1, False), 0)[1], 0)
     sig_out.wait_send()
     sig_share.wait_send()
-    for k in range(STAGES):
-        def sent(c, _, k=k):
-            for copy in halo_copies(k, c):
-                copy.wait_send()
-            return 0
-
-        lax.fori_loop(0, ncol, sent, 0)
+    lax.fori_loop(0, ncol, lambda c, _: (sent(ITERS, c), 0)[1], 0)
     every = parts.at[pl.ds(0, slabs - 1)]
     all_parts = remote(every, every, part_send, part_recv, right)
     all_parts.wait_recv()

time: 60.6 us -> 60.6 us (level)
  no operation moved by 1% of the time
where the time goes in v7:
time: 60.6 us; the launch traced here: 60.5 us
  Pallas kernels  59.8 us (99%)
  between operations  0.64 us (1%)
    pallas_call x1, Pallas kernels, shards(): pl.pallas_call(functools.partial(basis_kernel, (slabs, ncol, depth, rows)...  57.9 us
    pallas_call x1, Pallas kernels, shards(): pl.pallas_call(functools.partial(combine_kernel, (ncol, cells, rows)), ou...  1.96 us

profile of v7, /device:TPU:8, one launch (start us, length us, event | category | flops | bytes accessed | tf_op | source)
XLA Modules:
  0.0 60.5 jit_solution(16946291955700130016)
XLA Ops:
  0.6 57.9 %shard_map.59 = (f32[4,528,128]{2,1,0:T(8,128)S(1)}, f32[7,4,528,128]{3,2,1,0:T(8,128)S(1)}, f32[512,128]{1,0:T(8,128)S(1)}, f32[4,16,128]{2,1,0:T(8,128)S(1)}) custom-call(s32[8]{0:T(128)} %counts_hbm.1, s32[4,8]{1,0:T(4,128)} %bitcast.7, f32[512,128]{1,0:T(8,128)} %bitcast.6, f32[4,512,128]{2,1,0:T(8,128)} %bitcast.5), custom_call_target="tpu_custom_call" | custom-call | tf_op jit(solution)/shard_map/pallas_call | solution.py:467
  58.5 2.0 %shard_map.60 = (f32[4,512,128]{2,1,0:T(8,128)}, f32[4,512,128]{2,1,0:T(8,128)}) custom-call(f32[4,528,128]{2,1,0:T(8,128)S(1)} %get-tuple-element.8.x_in, f32[7,4,528,128]{3,2,1,0:T(8,128)S(1)} %get-tuple-element.9.v, f32[512,128]{1,0:T(8,128)S(1)} %get-tuple-element.10.diag, f32[4,16,128]{2,1,0:T(8,128)S(1)} %get-tuple-element.11.table), custom_call_target="tpu_custom_call" | custom-call | tf_op jit(solution)/shard_map/pallas_call | solution.py:508

commit v8 on v6

--- a/solution.py
+++ b/solution.py
@@ -265,11 +265,12 @@
         from_left.wait_recv()
         work(0, halo[k, 0, c], field(pl.ds(PAD + plane, plane)))
         if k == ITERS - 1:
-            pl.when(c != ncol - 2)(lambda: to_left.start())
+            pl.when((c == 0) | (c == ncol - 1))(lambda: to_left.start())
 
             @pl.when(c == ncol - 1)
             def _():
-                halo_copies(k + 1, ncol - 2)[1].start()
+                for late in range(1, ncol - 1):
+                    halo_copies(k + 1, late)[1].start()
 
         else:
             to_left.start()

time: 60.6 us -> 60.6 us (level)
  no operation moved by 1% of the time
where the time goes in v8:
time: 60.6 us; the launch traced here: 60.5 us
  Pallas kernels  59.8 us (99%)
  between operations  0.64 us (1%)
    pallas_call x1, Pallas kernels, shards(): pl.pallas_call(functools.partial(basis_kernel, (slabs, ncol, depth, rows)...  57.9 us
    pallas_call x1, Pallas kernels, shards(): pl.pallas_call(functools.partial(combine_kernel, (ncol, cells, rows)), ou...  1.96 us

profile of v8, /device:TPU:8, one launch (start us, length us, event | category | flops | bytes accessed | tf_op | source)
XLA Modules:
  0.0 60.5 jit_solution(648611069822799071)
XLA Ops:
  0.6 57.9 %shard_map.59 = (f32[4,528,128]{2,1,0:T(8,128)S(1)}, f32[7,4,528,128]{3,2,1,0:T(8,128)S(1)}, f32[512,128]{1,0:T(8,128)S(1)}, f32[4,16,128]{2,1,0:T(8,128)S(1)}) custom-call(s32[8]{0:T(128)} %counts_hbm.1, s32[4,8]{1,0:T(4,128)} %bitcast.7, f32[512,128]{1,0:T(8,128)} %bitcast.6, f32[4,512,128]{2,1,0:T(8,128)} %bitcast.5), custom_call_target="tpu_custom_call" | custom-call | tf_op jit(solution)/shard_map/pallas_call | solution.py:468
  58.5 2.0 %shard_map.60 = (f32[4,512,128]{2,1,0:T(8,128)}, f32[4,512,128]{2,1,0:T(8,128)}) custom-call(f32[4,528,128]{2,1,0:T(8,128)S(1)} %get-tuple-element.8.x_in, f32[7,4,528,128]{3,2,1,0:T(8,128)S(1)} %get-tuple-element.9.v, f32[512,128]{1,0:T(8,128)S(1)} %get-tuple-element.10.diag, f32[4,16,128]{2,1,0:T(8,128)S(1)} %get-tuple-element.11.table), custom_call_target="tpu_custom_call" | custom-call | tf_op jit(solution)/shard_map/pallas_call | solution.py:509
